TPU v7x, 32 devices: a whole 2x2x4 slice. The times are simulated.
32 devices in a mesh: section: 16 (over z, x, core), tensor: 2 (over y).
Axes of the slice: x: 2, y: 2, z: 4, core: 2. Of those that a mesh axis runs over, the one named last changes fastest.
Arguments:
- forward_input: bfloat16 [16, 256, 8192], P('section', None, 'tensor'), may hold values from -6 to 6
- saved_last: bfloat16 [16, 256, 8192], P('section', None, 'tensor'), may hold values from -6 to 6
- saved_first: bfloat16 [16, 256, 8192], P('section', None, 'tensor'), may hold values from -6 to 6
- first_cotangent: bfloat16 [16, 256, 8192], P('section', None, 'tensor'), may hold values from -6 to 6
- section_entry: bfloat16 [256, 8192], P(None, 'tensor'), may hold values from -6 to 6
- last_gain: float32 [16, 8192], P('section'), may hold values from 0.1 to 1.9
- last_up: bfloat16 [16, 8192, 1024], P('section', None, 'tensor'), may hold values from -0.0625 to 0.0625
- last_down: bfloat16 [16, 1024, 8192], P('section', 'tensor'), may hold values from -0.1875 to 0.1875
- first_gain: float32 [16, 8192], P('section'), may hold values from 0.1 to 1.9
- first_up: bfloat16 [16, 8192, 1024], P('section', None, 'tensor'), may hold values from -0.0625 to 0.0625
- first_down: bfloat16 [16, 1024, 8192], P('section', 'tensor'), may hold values from -0.1875 to 0.1875
- head_gain: float32 [8192], replicated, may hold values from 0.1 to 1.9
- head_weight: float32 [8192, 4], P('tensor'), may hold values from -0.0625 to 0.0625
- head_bias: float32 [4], replicated, may hold values from -3 to 3
- prompt_length: int32 [1], replicated, may hold values from 8 to 248
- keep_mask: int32 [1, 256], replicated, may hold values 0 or 1
- target_box: int32 [1, 4], replicated, may hold values from 0 to 1000, as said below
Outputs:
- layer_output: bfloat16 [16, 256, 8192], P('section', None, 'tensor')
- input_gradient: bfloat16 [16, 256, 8192], P('section', None, 'tensor')
Inputs may be any that keep to these rules, and one draw needn't show every extreme that they name: `target_box`: each row is a box x1, y1, x2, y2 with x2 - x1 and y2 - y1 at least 100.
All inputs are finite; a program needn't handle non-finite values.
Results may differ from a plain program's by a relative error of at most 0.018.
Values may be sent and summed in bfloat16 or wider, within the bound.
No kernel may reach another device: no remote copies, remote signals or barrier semaphores. Data moves between devices by JAX's collectives and lax.ppermute only.
A program may use at most 128 MiB of HBM per device.

v0:
```python
import functools

import jax
import jax.numpy as jnp
from jax import lax
from jax.experimental import pallas as pl
from jax.experimental.pallas import tpu as pltpu
from jax.sharding import PartitionSpec as P

epsilon = 1e-06
softness = 4.0
loss_scale = 4096.0
chunk_width = 1024

f32 = jnp.float32
bf16 = jnp.bfloat16


def shifted(value, axis, steps):
    count = lax.axis_size(axis)
    initial, last = (max(0, -steps), min(count, count - steps))
    return lax.ppermute(value, axis, [(source, source + steps) for source in range(initial, last)])


def rotated(value, steps):
    count = lax.axis_size("tensor")
    return lax.ppermute(value, "tensor", [(i, (i + steps) % count) for i in range(count)])


def fenced(value, after):
    return lax.optimization_barrier((value, *after))[0] if after else value


def copy_kernel(places, *refs):
    sources, targets, sems = refs[: -len(places) - 1], refs[-len(places) - 1 : -1], refs[-1]
    count, me = lax.axis_size("tensor"), lax.axis_index("tensor")
    copies = []
    for slot, (number, row, column) in enumerate(places):
        rows, columns = targets[slot].shape
        starts = []
        for size, (away, width, offset) in zip((rows, columns), (row, column)):
            start = offset if away is None else lax.rem(me + away, count) * width + offset
            starts.append(pl.ds(start if away is None else pl.multiple_of(start, 128), size))
        source = sources[number].at[starts[0], starts[1]]
        copies.append(pltpu.make_async_copy(source, targets[slot], sems.at[slot]))
    for copy in copies:
        copy.start()
    for copy in copies:
        copy.wait()


here = (None, 0, 0)


def copied(matrices, places, shapes):
    moved = sum(2 * rows * columns for rows, columns in shapes)
    anywhere = pl.BlockSpec(memory_space=pl.ANY)
    return pl.pallas_call(
        functools.partial(copy_kernel, places),
        out_shape=[jax.ShapeDtypeStruct(shape, bf16) for shape in shapes],
        in_specs=[anywhere] * len(matrices),
        out_specs=[pl.BlockSpec(memory_space=pltpu.VMEM)] * len(shapes),
        scratch_shapes=[pltpu.SemaphoreType.DMA((len(shapes),))],
        cost_estimate=pl.CostEstimate(flops=0, bytes_accessed=2 * moved, transcendentals=0),
        compiler_params=pltpu.CompilerParams(vmem_limit_bytes=32 * 1024 * 1024),
        name="copied",
    )(*matrices)


def settled(value):
    return lax.optimization_barrier(value)


def fenced_all(values, after):
    return lax.optimization_barrier((*values, *after))[: len(values)]


class Lane:
    def __init__(self, depth):
        self.depth = depth
        self.past = []

    def send(self, value, steps, after=(), depth=None):
        depth = depth or self.depth
        if len(self.past) >= depth:
            after = (self.past[-depth], *after)
        value = fenced(value, after)
        arrived = rotated(value, steps)
        self.past.append(arrived)
        return arrived


def dot(left, right):
    return jnp.dot(left, right, preferred_element_type=f32)


def dot_t(left, right):
    return lax.dot_general(left, right, (((1,), (1,)), ((), ())), preferred_element_type=f32)


def rows_at(matrix, start, size):
    return lax.dynamic_slice_in_dim(matrix, start, size, 0)


def cols_at(matrix, start, size):
    return lax.dynamic_slice_in_dim(matrix, start, size, 1)


def total(terms):
    result = terms[0]
    for term in terms[1:]:
        result = result + term
    return result


def soft_min(first, second):
    return 0.5 * (
        first + second - jnp.sqrt((first - second) * (first - second) + softness * softness)
    )


def soft_max(first, second):
    return 0.5 * (
        first + second + jnp.sqrt((first - second) * (first - second) + softness * softness)
    )


def soft_relu(difference):
    return 0.5 * (difference + jnp.sqrt(difference * difference + softness * softness))


def box_loss(logits, target):
    centre_x, centre_y, box_width, box_height = [jax.nn.sigmoid(v) * 1000.0 for v in logits]
    left, lower, right, upper = target
    left_pred = centre_x - 0.5 * box_width
    right_pred = centre_x + 0.5 * box_width
    lower_pred = centre_y - 0.5 * box_height
    upper_pred = centre_y + 0.5 * box_height
    inner_width = soft_relu(soft_min(right_pred, right) - soft_max(left_pred, left))
    inner_height = soft_relu(soft_min(upper_pred, upper) - soft_max(lower_pred, lower))
    intersection_area = inner_width * inner_height
    target_area = (right - left) * (upper - lower)
    union_area = box_width * box_height + target_area - intersection_area
    outer_width = soft_max(right_pred, right) - soft_min(left_pred, left)
    outer_height = soft_max(upper_pred, upper) - soft_min(lower_pred, lower)
    enclosing = outer_width * outer_height
    return 1.0 - intersection_area / union_area + (enclosing - union_area) / enclosing


def column(row):
    return jnp.transpose(jnp.broadcast_to(row, (128, row.shape[1])))[:, :1]


def gate_kernel(count, pairs, mine_ref, act_grad_ref, *refs):
    got_refs, refs = refs[: count - 1], refs[count - 1 :]
    left_refs, right_refs, refs = refs[:pairs], refs[pairs : 2 * pairs], refs[2 * pairs :]
    groups = mine_ref.shape[0] // act_grad_ref.shape[0]
    inverse_refs, (grad_ref, along_ref, *out_refs) = refs[:groups], refs[groups:]
    tokens = act_grad_ref.shape[0]
    pre = total([mine_ref[...]] + [ref[...].astype(f32) for ref in got_refs])
    first = pre[:tokens] * column(inverse_refs[0][...])
    gate = jax.nn.sigmoid(first)
    act_grad = total(
        [act_grad_ref[...]] + [dot_t(x[...], w[...]) for x, w in zip(left_refs, right_refs)]
    )
    grad = (act_grad * gate * (1.0 + first * (1.0 - gate))).astype(bf16)
    grad_ref[...] = grad
    along_ref[...] = lax.dot_general(
        jnp.ones((1, first.shape[1]), f32),
        grad.astype(f32) * first,
        (((1,), (1,)), ((), ())),
        precision=lax.Precision.HIGHEST,
        preferred_element_type=f32,
    )
    if groups > 1:
        second = pre[tokens:] * column(inverse_refs[1][...])
        out_refs[0][...] = (second * jax.nn.sigmoid(second)).astype(bf16)


def gated(mine, got, inverses, act_grad, left=(), right=()):
    tokens, hidden_width = act_grad.shape
    shapes = [
        jax.ShapeDtypeStruct((tokens, hidden_width), bf16),
        jax.ShapeDtypeStruct((1, tokens), f32),
    ]
    if mine.shape[0] > tokens:
        shapes.append(jax.ShapeDtypeStruct((mine.shape[0] - tokens, hidden_width), bf16))
    whole = pl.BlockSpec(memory_space=pltpu.VMEM)
    return pl.pallas_call(
        functools.partial(gate_kernel, len(got) + 1, len(left)),
        out_shape=shapes,
        in_specs=[whole] * (len(got) + 2 + 2 * len(left) + len(inverses)),
        out_specs=[whole] * len(shapes),
        compiler_params=pltpu.CompilerParams(vmem_limit_bytes=32 * 1024 * 1024),
        name="gated",
    )(mine, act_grad, *got, *left, *right, *inverses)


def head_kernel(count, full_width, *refs):
    pooled_refs, weight_refs = refs[:count], refs[count : 2 * count]
    gain_ref, bias_ref, target_ref, prompt_ref, keep_ref = refs[2 * count : 2 * count + 5]
    out_refs = refs[2 * count + 5 :]
    me = lax.axis_index("tensor")
    rows, width = pooled_refs[0].shape
    gains = []
    for k in range(count):
        start = pl.multiple_of(lax.rem(me + count - k, count) * width, width)
        gains.append(gain_ref[:, pl.ds(start, width)])
    for row in range(rows):
        weights = pool_weights(prompt_ref[row], keep_ref[row : row + 1, :])
        inverse_count = 1.0 / jnp.sum(weights, axis=1, keepdims=True)
        pooled = [ref[row : row + 1, :] * inverse_count for ref in pooled_refs]
        square = total([jnp.sum(p * p, axis=1, keepdims=True) for p in pooled])
        inverse = lax.rsqrt(square / full_width + epsilon)
        projected = inverse * total(
            [
                jnp.sum((p * g) * w[...], axis=1, keepdims=True)
                for p, g, w in zip(pooled, gains, weight_refs)
            ]
        )
        projected = [projected[j : j + 1, :] for j in range(4)]
        target = [target_ref[row, j].astype(f32) for j in range(4)]
        logits = [projected[j] + bias_ref[j] for j in range(4)]
        _, pullback = jax.vjp(lambda *values: box_loss(values, target), *logits)
        logit_grad = pullback(jnp.full((1, 1), loss_scale / rows, f32))
        row_mean = total([logit_grad[j] * projected[j] for j in range(4)]) / full_width
        for p, g, w, out in zip(pooled, gains, weight_refs, out_refs):
            scaled_grad = total([logit_grad[j] * w[j : j + 1, :] for j in range(4)])
            out[row : row + 1, :] = (
                inverse * (g * scaled_grad - p * inverse * row_mean) * inverse_count
            )


def pool_weights(prompt_length, keep_row):
    positions = lax.broadcasted_iota(jnp.int32, keep_row.shape, 1)
    starting = jnp.where(positions == prompt_length - 1, 1.0, 0.0)
    kept = jnp.where(positions >= prompt_length, 1.0, 0.0)
    return starting + kept * keep_row.astype(f32)


def head_rows(pooled, weights, head_gain, head_bias, target_box, prompt_length, keep_mask, full_width):
    count = len(pooled)
    whole = pl.BlockSpec(memory_space=pltpu.VMEM)
    scalars = pl.BlockSpec(memory_space=pltpu.SMEM)
    rows = pl.pallas_call(
        functools.partial(head_kernel, count, full_width),
        out_shape=[jax.ShapeDtypeStruct(p.shape, f32) for p in pooled],
        in_specs=[whole] * (2 * count + 1) + [scalars] * 3 + [whole],
        out_specs=[whole] * count,
        name="head",
    )(*pooled, *weights, head_gain[None, :], head_bias, target_box, prompt_length, keep_mask)
    return [row.astype(bf16) for row in rows]


def per_device(
    forward_input,
    saved_last,
    saved_first,
    first_cotangent,
    section_entry,
    last_gain,
    last_up,
    last_down,
    first_gain,
    first_up,
    first_down,
    head_gain,
    head_weight,
    head_bias,
    prompt_length,
    keep_mask,
    target_box,
):
    count = lax.axis_size("tensor")
    me = lax.axis_index("tensor")
    section_index = lax.axis_index("section")
    opening = section_index == 0
    closing = section_index == lax.axis_size("section") - 1
    entering, saved, cotangent = forward_input[0], saved_first[0], first_cotangent[0]
    last_up, last_down, first_up, first_down = last_up[0], last_down[0], first_up[0], first_down[0]
    tokens, width = entering.shape
    full_width = width * count
    hidden_width = last_up.shape[1]
    chunk = min(width, chunk_width)
    pieces = range(width // chunk)
    final = pieces[-1]
    others = range(1, count)
    after = [lax.rem(me + k, count) for k in range(count)]
    before = [lax.rem(me + count - k, count) for k in range(count)]

    def piece(values, j):
        return values[:, j * chunk : (j + 1) * chunk]

    def square_sum(values):
        values = values.astype(f32)
        return jnp.sum(values * values, axis=1)

    lane = Lane(2)
    first_gain_cols = rows_at(first_gain[0], me * width, width)
    last_gain_cols = rows_at(last_gain[0], me * width, width)

    def scaled(values, gain_cols):
        return (values.astype(f32) * gain_cols).astype(bf16)

    def gain_piece(gain_cols, j):
        return gain_cols[j * chunk : (j + 1) * chunk]

    def up_parts(up_matrix, sizes):
        starts = [sum(sizes[:cut]) for cut in range(len(sizes))]
        places = [(0, (k, width, start), here) for start in starts for k in others]
        shapes = [(size, hidden_width) for size in sizes for k in others]
        places.append((0, (0, width, 0), here))
        shapes.append((width, hidden_width))
        parts = copied([up_matrix], places, shapes)
        step = count - 1
        return [parts[i * step : (i + 1) * step] for i in range(len(sizes))], parts[-1]

    def down_parts(down_matrix):
        places = [(0, here, (k, width, 0)) for k in range(count)]
        return copied([down_matrix], places, [(hidden_width, width)] * count)

    def send_up(parts, ahead=(), depth=None):
        return [lane.send(part, k, ahead, depth) for part, k in zip(parts, others)]

    def up_rows(own, got, start, size):
        blocks = [own[start : start + size]]
        for cuts in zip(*got):
            taken, at = [], 0
            for cut in cuts:
                low, high = max(start - at, 0), min(start + size - at, cut.shape[0])
                if low < high:
                    taken.append(cut[low:high])
                at += cut.shape[0]
            blocks.append(taken[0] if len(taken) == 1 else jnp.concatenate(taken, axis=0))
        return blocks

    def exchange_cols(values, ahead=()):
        return [values] + [lane.send(values, k, ahead) for k in others]

    def sum_small(values):
        return total([values] + [rotated(values, k) for k in others])

    def collect(sent):
        return [lane.send(t, -k) for t, k in zip(sent, others)]

    def exchange_grad(pre_grad, along):
        blocks = [pre_grad] + [lane.send(pre_grad, k) for k in others]
        return blocks, sum_small(along)[0] / full_width

    def other_products(normed, got, after=()):
        sums = []
        for cuts in zip(*got):
            terms, at = [], 0
            for cut in cuts[:-1]:
                terms.append(dot(normed[:, at : at + cut.shape[0]], cut))
                at += cut.shape[0]
            early = [settled(total(terms))] if terms else []
            last = dot(fenced(normed[:, at:], [*early, *after]), cuts[-1])
            sums.append(total([*early, last]).astype(bf16))
        return sums

    def input_grad(values, given, inverse, gain_cols, blocks, along, up_blocks):
        norm_grad = total([dot_t(blocks[k], up_blocks[k]) for k in range(count)])
        unit = values.astype(f32) * inverse[:, None]
        return (
            given.astype(f32)
            + inverse[:, None] * (gain_cols * norm_grad - unit * along[:, None])
        ).astype(bf16)

    def send_out(activated, downs, j, ahead=()):
        values = [dot(activated, piece(downs[k], j)).astype(bf16) for k in others]
        return [lane.send(value, k, ahead) for value, k in zip(values, others)]

    def add_out(values, mine, terms):
        return (values.astype(f32) + total([mine] + [t.astype(f32) for t in terms])).astype(bf16)

    def act_grad_terms(blocks, downs):
        return [dot_t(blocks[k], downs[-k]) for k in range(count)]

    stored = jnp.where(closing, entering, saved_last[0])

    last_parts, last_up_own = up_parts(last_up, [width // 2] * 2)
    cotangents = exchange_cols(cotangent)
    last_got = [send_up(last_parts[0])]
    last_downs = down_parts(last_down)
    first_parts, first_up_own = up_parts(first_up, [width // 4, width // 4, width // 2])
    first_downs = down_parts(first_down)
    squares = jnp.stack([square_sum(saved), square_sum(entering), square_sum(stored)])
    head_weights = [head_weight.T]
    entering_scaled = scaled(entering, last_gain_cols)
    stored_scaled = scaled(stored, last_gain_cols)
    first_saved = scaled(saved, first_gain_cols)

    last_got.append(send_up(last_parts[1]))
    ahead = [
        *last_downs, first_up_own, *first_downs, squares, *head_weights, entering_scaled,
        stored_scaled, first_saved,
    ]
    first_got = [send_up(first_parts[0], ahead)]
    sent = other_products(entering_scaled, last_got)
    mine = dot(fenced(entering_scaled, sent), last_up_own)
    got = collect(sent)
    squares = fenced(squares, sent)
    squares = total([squares] + [rotated(squares, k) for k in others])
    inverses = lax.rsqrt(squares / full_width + epsilon)
    head_weights += [rotated(fenced(head_weights[0], sent), k) for k in others]
    act_grad = total(act_grad_terms(cotangents, first_downs))
    first_got.append(send_up(first_parts[1], sent))
    stored_sent = other_products(fenced(stored_scaled, sent), last_got)
    stored_mine = dot(fenced(stored_scaled, sent), last_up_own)
    stored_got = collect(stored_sent)
    inverse_rows = [settled(inverses[i : i + 1]) for i in range(3)]
    first_gains = [settled(gain_piece(first_gain_cols, j)) for j in pieces]
    last_up_got = [settled(jnp.concatenate(cuts, axis=0)) for cuts in zip(*last_got)]
    right = [settled(piece(last_downs[-k], final)) for k in others]
    got = fenced_all(got, [*right, *last_up_got, *stored_sent, stored_mine, act_grad, *inverse_rows, *first_gains, last_gain_cols, *head_weights[1:]])
    entering_pre = total([mine] + [t.astype(f32) for t in got]) * inverses[1][:, None]

    activated = jax.nn.silu(entering_pre).astype(bf16)
    gots = [send_out(activated, last_downs, j) for j in pieces[:-1]]
    mine = dot(activated, last_downs[0])
    gots.append(send_out(activated, last_downs, final, [mine]))
    first_got.append(send_up(first_parts[2], depth=3))
    hidden = add_out(entering, mine, [jnp.concatenate(t, axis=1) for t in zip(*gots)])
    entry = jnp.where(opening, section_entry, shifted(hidden, "section", 1))

    row_count, row_length = keep_mask.shape
    token_weights = jnp.concatenate(
        [pool_weights(prompt_length[row], keep_mask[row : row + 1]) for row in range(row_count)], 0
    )

    def pool(values):
        weights = token_weights.astype(bf16)
        if row_count == 1:
            return dot(weights, values)
        values = values.reshape(row_count, row_length, values.shape[1])
        return jnp.einsum("rt,rtd->rd", weights, values, preferred_element_type=f32)

    def on_tokens(rows):
        values = token_weights[:, :, None] * rows.astype(f32)[:, None, :]
        return values.reshape(tokens, rows.shape[1])

    pooled = pool(fenced(hidden, [entry]))
    pooled = [pooled] + [rotated(pooled, k) for k in others]

    entry_squares = sum_small(square_sum(entry)[None, :])
    entry_inverse = settled(lax.rsqrt(entry_squares / full_width + epsilon))
    pair = jnp.concatenate([first_saved, scaled(entry, first_gain_cols)], axis=0)
    sent = other_products(pair, first_got, [entry_inverse])
    mine = dot(fenced(pair, sent), first_up_own)
    got = collect(sent)

    pre_grad, along, entry_activated = gated(mine, got, [inverse_rows[0], entry_inverse], act_grad)
    first_blocks, first_along = exchange_grad(pre_grad, along)
    early = (len(pieces) + 1) // 2

    def first_out(low, high, activated):
        columns = slice(low * chunk, high * chunk)
        values = [dot(activated, first_downs[k][:, columns]).astype(bf16) for k in others]
        return [lane.send(value, k) for value, k in zip(values, others)]

    gots = [first_out(0, early, entry_activated)]
    returned = []
    for j in pieces:
        gradient = input_grad(
            piece(saved, j),
            piece(cotangent, j),
            inverses[0],
            first_gains[j],
            fenced_all(first_blocks, returned[-1:]),
            first_along,
            up_rows(first_up_own, first_got, j * chunk, chunk),
        )
        returned.append(gradient)
    returned = [shifted(gradient, "section", -1) for gradient in returned]

    act_grads = []
    for j in pieces[:-1]:
        ahead = act_grads[j - 2 : j - 1] if j > 1 else ()
        blocks = exchange_cols(returned[j], ahead)
        terms = act_grad_terms(blocks, [piece(d, j) for d in last_downs])
        act_grads.append(total(act_grads[-1:] + terms))
        if j == 0:
            late = blocks[1:]
    if final == 0:
        late = first_blocks[1:]
    head_grads = head_rows(
        fenced_all(pooled, late),
        head_weights,
        head_gain,
        head_bias,
        target_box,
        prompt_length,
        keep_mask,
        full_width,
    )
    head_act_grad = total([dot_t(head_grads[k], last_downs[-k]) for k in range(count)])
    given = settled(
        jnp.where(
            closing, on_tokens(head_grads[0]).astype(bf16), jnp.concatenate(returned, axis=1)
        )
    )
    act_grad = settled(
        total(
            [
                jnp.where(closing, on_tokens(head_act_grad), 0.0),
                dot_t(returned[-1], piece(last_downs[0], final)),
                *act_grads[-1:],
            ]
        )
    )
    activated_late = fenced(entry_activated, late)
    if early < final:
        gots.append(first_out(early, final, activated_late))
    ahead = [given, act_grad, *right, *(gots[-1] if early < final else ())]
    left = exchange_cols(returned[-1], ahead)[1:]
    pre_grad, along = gated(stored_mine, stored_got, inverse_rows[2:], act_grad, left, right)
    last_blocks, last_along = exchange_grad(pre_grad, along)
    if early <= final:
        gots.append(first_out(max(early, final), len(pieces), activated_late))
    outs, at = [], 0
    for got in gots[:-1]:
        columns = slice(at, at + got[0].shape[1])
        mine = dot(activated_late, first_downs[0][:, columns])
        outs.append(add_out(entry[:, columns], mine, got))
        at = columns.stop
    mine = settled(dot(activated_late, first_downs[0][:, at:]))
    outs = jnp.concatenate([*outs, entry[:, at:]], axis=1)
    got = fenced_all(gots[-1], [mine, outs])
    layer_output = lax.dynamic_update_slice_in_dim(outs, add_out(entry[:, at:], mine, got), at, 1)

    own = settled(dot_t(last_blocks[0], last_up_own))
    norm_grad = total(
        [own] + [dot_t(block, got) for block, got in zip(last_blocks[1:], last_up_got)]
    )
    unit = stored.astype(f32) * inverses[2][:, None]
    input_gradient = (
        given.astype(f32)
        + inverses[2][:, None] * (last_gain_cols * norm_grad - unit * last_along[:, None])
    ).astype(bf16)
    return (layer_output[None], input_gradient[None])


def solution(mesh):
    placed = (
        P("section", None, "tensor"),
        P("section", None, "tensor"),
        P("section", None, "tensor"),
        P("section", None, "tensor"),
        P(None, "tensor"),
        P("section", None),
        P("section", None, "tensor"),
        P("section", "tensor", None),
        P("section", None),
        P("section", None, "tensor"),
        P("section", "tensor", None),
        P(),
        P("tensor", None),
        P(),
        P(),
        P(),
        P(),
    )
    return jax.shard_map(
        per_device,
        mesh=mesh,
        in_specs=placed,
        out_specs=(P("section", None, "tensor"), P("section", None, "tensor")),
        check_vma=False,
    )
```

profile of v0, /device:TPU:16, one launch (start us, length us, event | category | flops | bytes accessed | tf_op | source)
XLA Modules:
  0.0 421.9 jit_solution(2821692600153852850)
XLA Ops:
  11.4 5.0 %fusion.8 = (f32[256]{0:T(256)S(1)}, bf16[1,256,4096]{2,1,0:T(8,128)(2,1)}, f32[256]{0:T(256)S(1)}, bf16[256,4096]{1,0:T(8,128)(2,1)S(1)}) fusion(bf16[1,256,4096]{2,1,0:T(8,128)(2,1)} %param.17, bf16[1,256,4096]{2,1,0:T(8,128)(2,1)} %param.18, pred[]{:T(512)S(6)} %eq.21, f32[4096]{0:T(1024)S(1)} %bitcast.129), kind=kLoop, calls=%fused_computation.25 | loop fusion | flops 9436672 | bytes 8407041 | tf_op jit(solution)/shard_map/reduce_sum | solution.py:296
  18.8 3.4 copy-done.6
  30.5 4.1 copy-done.8
  38.3 11.3 %collective-permute-done.1 = bf16[256,4096]{1,0:T(8,128)(2,1)} collective-permute-done((bf16[256,4096]{1,0:T(8,128)(2,1)}, bf16[256,4096]{1,0:T(8,128)(2,1)}, u32[]{:S(2)}, u32[]{:S(2)}) %collective-permute-start.1) | collective-permute-done | bytes 2097184 | tf_op jit(solution)/shard_map/ppermute | solution.py:27
  52.9 41.6 %collective-permute-done = bf16[2048,512]{1,0:T(8,128)(2,1)} collective-permute-done((bf16[2048,512]{1,0:T(8,128)(2,1)}, bf16[2048,512]{1,0:T(8,128)(2,1)}, u32[]{:S(2)}, u32[]{:S(2)}) %collective-permute-start) | collective-permute-done | bytes 2097184 | tf_op jit(solution)/shard_map/ppermute | solution.py:27
  101.3 38.0 %collective-permute-done.2 = bf16[2048,512]{1,0:T(8,128)(2,1)S(1)} collective-permute-done((bf16[2048,512]{1,0:T(8,128)(2,1)S(1)}, bf16[2048,512]{1,0:T(8,128)(2,1)S(1)}, u32[]{:S(2)}, u32[]{:S(2)}) %collective-permute-start.2) | collective-permute-done | bytes 2097184 | tf_op jit(solution)/shard_map/ppermute | solution.py:27
  148.6 13.2 %collective-permute-done.6 = bf16[1024,512]{1,0:T(8,128)(2,1)S(1)} collective-permute-done((bf16[1024,512]{1,0:T(8,128)(2,1)S(1)}, bf16[1024,512]{1,0:T(8,128)(2,1)S(1)}, u32[]{:S(2)}, u32[]{:S(2)}) %collective-permute-start.6) | collective-permute-done | bytes 1048608 | tf_op jit(solution)/shard_map/ppermute | solution.py:27
  163.3 3.8 pad_maximum_fusion.1
  172.0 23.8 %collective-permute-done.9.refs_0_ = bf16[256,512]{1,0:T(8,128)(2,1)S(1)} collective-permute-done((bf16[256,512]{1,0:T(8,128)(2,1)S(1)}, bf16[256,512]{1,0:T(8,128)(2,1)S(1)}, u32[]{:S(2)}, u32[]{:S(2)}) %collective-permute-start.9) | collective-permute-done | bytes 262176 | tf_op jit(solution)/shard_map/ppermute | solution.py:27
  199.6 11.1 %collective-permute-done.10 = bf16[256,1024]{1,0:T(8,128)(2,1)S(1)} collective-permute-done((bf16[256,1024]{1,0:T(8,128)(2,1)S(1)}, bf16[256,1024]{1,0:T(8,128)(2,1)S(1)}, u32[]{:S(2)}, u32[]{:S(2)}) %collective-permute-start.10) | collective-permute-done | bytes 524320 | tf_op jit(solution)/shard_map/ppermute | solution.py:27
  212.2 9.7 %collective-permute-done.8 = bf16[256,1024]{1,0:T(8,128)(2,1)S(1)} collective-permute-done((bf16[256,1024]{1,0:T(8,128)(2,1)S(1)}, bf16[256,1024]{1,0:T(8,128)(2,1)S(1)}, u32[]{:S(2)}, u32[]{:S(2)}) %collective-permute-start.8) | collective-permute-done | bytes 524320 | tf_op jit(solution)/shard_map/ppermute | solution.py:27
  223.5 9.7 %collective-permute-done.12 = bf16[256,1024]{1,0:T(8,128)(2,1)S(1)} collective-permute-done((bf16[256,1024]{1,0:T(8,128)(2,1)S(1)}, bf16[256,1024]{1,0:T(8,128)(2,1)S(1)}, u32[]{:S(2)}, u32[]{:S(2)}) %collective-permute-start.12) | collective-permute-done | bytes 524320 | tf_op jit(solution)/shard_map/ppermute | solution.py:27
  233.2 9.2 %collective-permute-done.11 = bf16[256,1024]{1,0:T(8,128)(2,1)S(1)} collective-permute-done((bf16[256,1024]{1,0:T(8,128)(2,1)S(1)}, bf16[256,1024]{1,0:T(8,128)(2,1)S(1)}, u32[]{:S(2)}, u32[]{:S(2)}) %collective-permute-start.11) | collective-permute-done | bytes 524320 | tf_op jit(solution)/shard_map/ppermute | solution.py:27
  248.5 24.2 %collective-permute-done.13 = bf16[256,4096]{1,0:T(8,128)(2,1)} collective-permute-done((bf16[256,4096]{1,0:T(8,128)(2,1)}, bf16[256,4096]{1,0:T(8,128)(2,1)}, u32[]{:S(2)}, u32[]{:S(2)}) %collective-permute-start.13) | collective-permute-done | bytes 2097184 | tf_op jit(solution)/shard_map/ppermute | solution.py:22
  283.0 12.5 %collective-permute-done.14 = f32[1,256]{1,0:T(1,128)S(1)} collective-permute-done((f32[1,256]{1,0:T(1,128)S(1)}, f32[1,256]{1,0:T(1,128)S(1)}, u32[]{:S(2)}, u32[]{:S(2)}) %collective-permute-start.14) | collective-permute-done | bytes 1056 | tf_op jit(solution)/shard_map/ppermute | solution.py:27
  300.8 10.3 %collective-permute-done.16.refs_0_ = bf16[512,512]{1,0:T(8,128)(2,1)S(1)} collective-permute-done((bf16[512,512]{1,0:T(8,128)(2,1)S(1)}, bf16[512,512]{1,0:T(8,128)(2,1)S(1)}, u32[]{:S(2)}, u32[]{:S(2)}) %collective-permute-start.16) | collective-permute-done | bytes 524320 | tf_op jit(solution)/shard_map/ppermute | solution.py:27
  316.4 6.4 %collective-permute-done.17 = bf16[256,512]{1,0:T(8,128)(2,1)S(1)} collective-permute-done((bf16[256,512]{1,0:T(8,128)(2,1)S(1)}, bf16[256,512]{1,0:T(8,128)(2,1)S(1)}, u32[]{:S(2)}, u32[]{:S(2)}) %collective-permute-start.17) | collective-permute-done | bytes 262176 | tf_op jit(solution)/shard_map/ppermute | solution.py:27
  336.1 7.7 %collective-permute-done.26 = bf16[256,1024]{1,0:T(8,128)(2,1)} collective-permute-done((bf16[256,1024]{1,0:T(8,128)(2,1)S(1)}, bf16[256,1024]{1,0:T(8,128)(2,1)}, u32[]{:S(2)}, u32[]{:S(2)}) %collective-permute-start.26) | collective-permute-done | bytes 524320 | tf_op jit(solution)/shard_map/ppermute | solution.py:22
  343.8 5.1 %collective-permute-start.25 = (bf16[256,1024]{1,0:T(8,128)(2,1)}, bf16[256,1024]{1,0:T(8,128)(2,1)}, u32[]{:S(2)}, u32[]{:S(2)}) collective-permute-start(bf16[256,1024]{1,0:T(8,128)(2,1)} %fusion.38), channel_id=1, source_target_pairs={{2,0},{4,2},{6,4},{8,6},{10,8},{12,10},{14,12},{16,14},{18,16},{20... | collective-permute-start | bytes 1572872 | tf_op jit(solution)/shard_map/ppermute | solution.py:22
  351.8 4.6 %collective-permute-done.20 = bf16[256,1024]{1,0:T(8,128)(2,1)S(1)} collective-permute-done((bf16[256,1024]{1,0:T(8,128)(2,1)S(1)}, bf16[256,1024]{1,0:T(8,128)(2,1)S(1)}, u32[]{:S(2)}, u32[]{:S(2)}) %collective-permute-start.20) | collective-permute-done | bytes 524320 | tf_op jit(solution)/shard_map/ppermute | solution.py:27
  362.0 3.7 fusion.86
  383.7 4.9 %collective-permute-done.24 = bf16[256,1024]{1,0:T(8,128)(2,1)S(1)} collective-permute-done((bf16[256,1024]{1,0:T(8,128)(2,1)S(1)}, bf16[256,1024]{1,0:T(8,128)(2,1)S(1)}, u32[]{:S(2)}, u32[]{:S(2)}) %collective-permute-start.24) | collective-permute-done | bytes 524320 | tf_op jit(solution)/shard_map/ppermute | solution.py:27
  389.6 11.6 %collective-permute-done.29.refs_1_ = bf16[256,1024]{1,0:T(8,128)(2,1)S(1)} collective-permute-done((bf16[256,1024]{1,0:T(8,128)(2,1)}, bf16[256,1024]{1,0:T(8,128)(2,1)S(1)}, u32[]{:S(2)}, u32[]{:S(2)}) %collective-permute-start.29) | collective-permute-done | bytes 524320 | tf_op jit(solution)/shard_map/ppermute | solution.py:27
  406.5 5.8 %collective-permute-done.31 = bf16[256,512]{1,0:T(8,128)(2,1)S(1)} collective-permute-done((bf16[256,512]{1,0:T(8,128)(2,1)S(1)}, bf16[256,512]{1,0:T(8,128)(2,1)S(1)}, u32[]{:S(2)}, u32[]{:S(2)}) %collective-permute-start.31) | collective-permute-done | bytes 262176 | tf_op jit(solution)/shard_map/ppermute | solution.py:27
  (244 shorter events, 138.6 us)
Async XLA Ops:
  0.6 48.9 %collective-permute-start.1 = (bf16[256,4096]{1,0:T(8,128)(2,1)}, bf16[256,4096]{1,0:T(8,128)(2,1)}, u32[]{:S(2)}, u32[]{:S(2)}) collective-permute-start(bf16[256,4096]{1,0:T(8,128)(2,1)} %bitcast.156), channel_id=1, source_target_pairs={{0,1},{1,0},{2,3},{3,2},{4,5},{5,4},{6,7},{7,6},{8,9},{9,8},{10,11... | collective-permute-start | bytes 6291464 | tf_op jit(solution)/shard_map/ppermute | solution.py:27
  10.9 83.6 %collective-permute-start = (bf16[2048,512]{1,0:T(8,128)(2,1)}, bf16[2048,512]{1,0:T(8,128)(2,1)}, u32[]{:S(2)}, u32[]{:S(2)}) collective-permute-start(bf16[2048,512]{1,0:T(8,128)(2,1)} %get-tuple-element.62), channel_id=1, source_target_pairs={{0,1},{1,0},{2,3},{3,2},{4,5},{5,4},{6,7},{7,6},{8,9},{9,8},{10,11... | collective-permute-start | bytes 6291464 | tf_op jit(solution)/shard_map/ppermute | solution.py:27
  49.5 89.8 %collective-permute-start.2 = (bf16[2048,512]{1,0:T(8,128)(2,1)S(1)}, bf16[2048,512]{1,0:T(8,128)(2,1)S(1)}, u32[]{:S(2)}, u32[]{:S(2)}) collective-permute-start(bf16[2048,512]{1,0:T(8,128)(2,1)S(1)} %copy-done.26), channel_id=1, source_target_pairs={{0,1},{1,0},{2,3},{3,2},{4,5},{5,4},{6,7},{7,6},{8,9},{9,8},{10,11... | collective-permute-start | bytes 6291464 | tf_op jit(solution)/shard_map/ppermute | solution.py:27
  96.8 65.0 %collective-permute-start.6 = (bf16[1024,512]{1,0:T(8,128)(2,1)S(1)}, bf16[1024,512]{1,0:T(8,128)(2,1)S(1)}, u32[]{:S(2)}, u32[]{:S(2)}) collective-permute-start(bf16[1024,512]{1,0:T(8,128)(2,1)S(1)} %get-tuple-element.81), channel_id=1, source_target_pairs={{0,1},{1,0},{2,3},{3,2},{4,5},{5,4},{6,7},{7,6},{8,9},{9,8},{10,11... | collective-permute-start | bytes 3145736 | tf_op jit(solution)/shard_map/ppermute | solution.py:27
  142.4 25.5 %collective-permute-start.4 = (f32[3,256]{1,0:T(4,128)S(1)}, f32[3,256]{1,0:T(4,128)S(1)}, u32[]{:S(2)}, u32[]{:S(2)}) collective-permute-start(f32[3,256]{1,0:T(4,128)S(1)} %pad_maximum_fusion.3), channel_id=1, source_target_pairs={{0,1},{1,0},{2,3},{3,2},{4,5},{5,4},{6,7},{7,6},{8,9},{9,8},{10,11... | collective-permute-start | bytes 9224 | tf_op jit(solution)/shard_map/ppermute | solution.py:27
  143.9 25.0 %collective-permute-start.3 = (bf16[256,512]{1,0:T(8,128)(2,1)S(1)}, bf16[256,512]{1,0:T(8,128)(2,1)S(1)}, u32[]{:S(2)}, u32[]{:S(2)}) collective-permute-start(bf16[256,512]{1,0:T(8,128)(2,1)S(1)} %fusion.44), channel_id=1, source_target_pairs={{0,1},{1,0},{2,3},{3,2},{4,5},{5,4},{6,7},{7,6},{8,9},{9,8},{10,11... | collective-permute-start | bytes 786440 | tf_op jit(solution)/shard_map/ppermute | solution.py:27
  144.5 24.5 %collective-permute-start.5 = (f32[4,4096]{1,0:T(4,128)S(1)}, f32[4,4096]{1,0:T(4,128)S(1)}, u32[]{:S(2)}, u32[]{:S(2)}) collective-permute-start(f32[4,4096]{1,0:T(4,128)S(1)} %bitcast.135), channel_id=1, source_target_pairs={{0,1},{1,0},{2,3},{3,2},{4,5},{5,4},{6,7},{7,6},{8,9},{9,8},{10,11... | collective-permute-start | bytes 196616 | tf_op jit(solution)/shard_map/ppermute | solution.py:27
  161.8 35.6 %collective-permute-start.7 = (bf16[1024,512]{1,0:T(8,128)(2,1)S(1)}, bf16[1024,512]{1,0:T(8,128)(2,1)S(1)}, u32[]{:S(2)}, u32[]{:S(2)}) collective-permute-start(bf16[1024,512]{1,0:T(8,128)(2,1)S(1)} %get-tuple-element.82), channel_id=1, source_target_pairs={{0,1},{1,0},{2,3},{3,2},{4,5},{5,4},{6,7},{7,6},{8,9},{9,8},{10,11... | collective-permute-start | bytes 3145736 | tf_op jit(solution)/shard_map/ppermute | solution.py:27
  168.9 26.9 %collective-permute-start.9 = (bf16[256,512]{1,0:T(8,128)(2,1)S(1)}, bf16[256,512]{1,0:T(8,128)(2,1)S(1)}, u32[]{:S(2)}, u32[]{:S(2)}) collective-permute-start(bf16[256,512]{1,0:T(8,128)(2,1)S(1)} %fusion.45), channel_id=1, source_target_pairs={{0,1},{1,0},{2,3},{3,2},{4,5},{5,4},{6,7},{7,6},{8,9},{9,8},{10,11... | collective-permute-start | bytes 786440 | tf_op jit(solution)/shard_map/ppermute | solution.py:27
  195.8 14.9 %collective-permute-start.10 = (bf16[256,1024]{1,0:T(8,128)(2,1)S(1)}, bf16[256,1024]{1,0:T(8,128)(2,1)S(1)}, u32[]{:S(2)}, u32[]{:S(2)}) collective-permute-start(bf16[256,1024]{1,0:T(8,128)(2,1)S(1)} %convolution_convert_fusion.5), channel_id=1, source_target_pairs={{0,1},{1,0},{2,3},{3,2},{4,5},{5,4},{6,7},{7,6},{8,9},{9,8},{10,11... | collective-permute-start | bytes 1572872 | tf_op jit(solution)/shard_map/ppermute | solution.py:27
  197.4 24.6 %collective-permute-start.8 = (bf16[256,1024]{1,0:T(8,128)(2,1)S(1)}, bf16[256,1024]{1,0:T(8,128)(2,1)S(1)}, u32[]{:S(2)}, u32[]{:S(2)}) collective-permute-start(bf16[256,1024]{1,0:T(8,128)(2,1)S(1)} %convolution_convert_fusion.6), channel_id=1, source_target_pairs={{0,1},{1,0},{2,3},{3,2},{4,5},{5,4},{6,7},{7,6},{8,9},{9,8},{10,11... | collective-permute-start | bytes 1572872 | tf_op jit(solution)/shard_map/ppermute | solution.py:27
  210.7 22.5 %collective-permute-start.12 = (bf16[256,1024]{1,0:T(8,128)(2,1)S(1)}, bf16[256,1024]{1,0:T(8,128)(2,1)S(1)}, u32[]{:S(2)}, u32[]{:S(2)}) collective-permute-start(bf16[256,1024]{1,0:T(8,128)(2,1)S(1)} %convolution_convert_fusion.3), channel_id=1, source_target_pairs={{0,1},{1,0},{2,3},{3,2},{4,5},{5,4},{6,7},{7,6},{8,9},{9,8},{10,11... | collective-permute-start | bytes 1572872 | tf_op jit(solution)/shard_map/ppermute | solution.py:27
  221.9 20.4 %collective-permute-start.11 = (bf16[256,1024]{1,0:T(8,128)(2,1)S(1)}, bf16[256,1024]{1,0:T(8,128)(2,1)S(1)}, u32[]{:S(2)}, u32[]{:S(2)}) collective-permute-start(bf16[256,1024]{1,0:T(8,128)(2,1)S(1)} %convolution_convert_fusion.4), channel_id=1, source_target_pairs={{0,1},{1,0},{2,3},{3,2},{4,5},{5,4},{6,7},{7,6},{8,9},{9,8},{10,11... | collective-permute-start | bytes 1572872 | tf_op jit(solution)/shard_map/ppermute | solution.py:27
  244.1 28.6 %collective-permute-start.13 = (bf16[256,4096]{1,0:T(8,128)(2,1)}, bf16[256,4096]{1,0:T(8,128)(2,1)}, u32[]{:S(2)}, u32[]{:S(2)}) collective-permute-start(bf16[256,4096]{1,0:T(8,128)(2,1)} %fusion.6), channel_id=1, source_target_pairs={{0,2},{2,4},{4,6},{6,8},{8,10},{10,12},{12,14},{14,16},{16,18},{18... | collective-permute-start | bytes 6291464 | tf_op jit(solution)/shard_map/ppermute | solution.py:22
  246.9 48.6 %collective-permute-start.15 = (bf16[2048,512]{1,0:T(8,128)(2,1)}, bf16[2048,512]{1,0:T(8,128)(2,1)S(1)}, u32[]{:S(2)}, u32[]{:S(2)}) collective-permute-start(bf16[2048,512]{1,0:T(8,128)(2,1)} %copy-done.24), channel_id=1, source_target_pairs={{0,1},{1,0},{2,3},{3,2},{4,5},{5,4},{6,7},{7,6},{8,9},{9,8},{10,11... | collective-permute-start | bytes 6291464 | tf_op jit(solution)/shard_map/ppermute | solution.py:27
  278.8 73.0 %collective-permute-start.28 = (f32[1,4096]{1,0:T(1,128)S(1)}, f32[1,4096]{1,0:T(1,128)S(1)}, u32[]{:S(2)}, u32[]{:S(2)}) collective-permute-start(f32[1,4096]{1,0:T(1,128)S(1)} %fusion.92.refs_0_), channel_id=1, source_target_pairs={{0,1},{1,0},{2,3},{3,2},{4,5},{5,4},{6,7},{7,6},{8,9},{9,8},{10,11... | collective-permute-start | bytes 49160 | tf_op jit(solution)/shard_map/ppermute | solution.py:27
  280.3 15.2 %collective-permute-start.14 = (f32[1,256]{1,0:T(1,128)S(1)}, f32[1,256]{1,0:T(1,128)S(1)}, u32[]{:S(2)}, u32[]{:S(2)}) collective-permute-start(f32[1,256]{1,0:T(1,128)S(1)} %bitcast.150), channel_id=1, source_target_pairs={{0,1},{1,0},{2,3},{3,2},{4,5},{5,4},{6,7},{7,6},{8,9},{9,8},{10,11... | collective-permute-start | bytes 3080 | tf_op jit(solution)/shard_map/ppermute | solution.py:27
  314.8 36.4 %collective-permute-start.21 = (bf16[256,2048]{1,0:T(8,128)(2,1)S(1)}, bf16[256,2048]{1,0:T(8,128)(2,1)S(1)}, u32[]{:S(2)}, u32[]{:S(2)}) collective-permute-start(bf16[256,2048]{1,0:T(8,128)(2,1)S(1)} %convolution_convert_fusion), channel_id=1, source_target_pairs={{0,1},{1,0},{2,3},{3,2},{4,5},{5,4},{6,7},{7,6},{8,9},{9,8},{10,11... | collective-permute-start | bytes 3145736 | tf_op jit(solution)/shard_map/ppermute | solution.py:27
  327.0 24.3 %collective-permute-start.22 = (bf16[256,1024]{1,0:T(8,128)(2,1)S(1)}, bf16[256,1024]{1,0:T(8,128)(2,1)}, u32[]{:S(2)}, u32[]{:S(2)}) collective-permute-start(bf16[256,1024]{1,0:T(8,128)(2,1)S(1)} %fusion.36), channel_id=1, source_target_pairs={{2,0},{4,2},{6,4},{8,6},{10,8},{12,10},{14,12},{16,14},{18,16},{20... | collective-permute-start | bytes 1572872 | tf_op jit(solution)/shard_map/ppermute | solution.py:22
  334.1 22.3 %collective-permute-start.20 = (bf16[256,1024]{1,0:T(8,128)(2,1)S(1)}, bf16[256,1024]{1,0:T(8,128)(2,1)S(1)}, u32[]{:S(2)}, u32[]{:S(2)}) collective-permute-start(bf16[256,1024]{1,0:T(8,128)(2,1)S(1)} %collective-permute-done.19), channel_id=1, source_target_pairs={{0,1},{1,0},{2,3},{3,2},{4,5},{5,4},{6,7},{7,6},{8,9},{9,8},{10,11... | collective-permute-start | bytes 1572872 | tf_op jit(solution)/shard_map/ppermute | solution.py:27
  343.8 23.2 %collective-permute-start.25 = (bf16[256,1024]{1,0:T(8,128)(2,1)}, bf16[256,1024]{1,0:T(8,128)(2,1)}, u32[]{:S(2)}, u32[]{:S(2)}) collective-permute-start(bf16[256,1024]{1,0:T(8,128)(2,1)} %fusion.38), channel_id=1, source_target_pairs={{2,0},{4,2},{6,4},{8,6},{10,8},{12,10},{14,12},{16,14},{18,16},{20... | collective-permute-start | bytes 1572872 | tf_op jit(solution)/shard_map/ppermute | solution.py:22
  351.3 22.1 %collective-permute-start.23 = (bf16[256,1024]{1,0:T(8,128)(2,1)}, bf16[256,1024]{1,0:T(8,128)(2,1)}, u32[]{:S(2)}, u32[]{:S(2)}) collective-permute-start(bf16[256,1024]{1,0:T(8,128)(2,1)} %collective-permute-done.22), channel_id=1, source_target_pairs={{0,1},{1,0},{2,3},{3,2},{4,5},{5,4},{6,7},{7,6},{8,9},{9,8},{10,11... | collective-permute-start | bytes 1572872 | tf_op jit(solution)/shard_map/ppermute | solution.py:27
  358.7 20.3 %collective-permute-start.27 = (bf16[256,1024]{1,0:T(8,128)(2,1)}, bf16[256,1024]{1,0:T(8,128)(2,1)}, u32[]{:S(2)}, u32[]{:S(2)}) collective-permute-start(bf16[256,1024]{1,0:T(8,128)(2,1)} %collective-permute-done.26), channel_id=1, source_target_pairs={{0,1},{1,0},{2,3},{3,2},{4,5},{5,4},{6,7},{7,6},{8,9},{9,8},{10,11... | collective-permute-start | bytes 1572872 | tf_op jit(solution)/shard_map/ppermute | solution.py:27
  373.4 15.2 %collective-permute-start.24 = (bf16[256,1024]{1,0:T(8,128)(2,1)S(1)}, bf16[256,1024]{1,0:T(8,128)(2,1)S(1)}, u32[]{:S(2)}, u32[]{:S(2)}) collective-permute-start(bf16[256,1024]{1,0:T(8,128)(2,1)S(1)} %convolution_convert_fusion.2), channel_id=1, source_target_pairs={{0,1},{1,0},{2,3},{3,2},{4,5},{5,4},{6,7},{7,6},{8,9},{9,8},{10,11... | collective-permute-start | bytes 1572872 | tf_op jit(solution)/shard_map/ppermute | solution.py:27
  (70 other events, 1223.0 us)
where the time goes:
time: 426 us; the launch traced here: 422 us
  waiting for transfers between devices  262 us (62%)
  matrix products  50.7 us (12%)
  starting transfers between devices  46.7 us (11%)
  other arithmetic  24.4 us (6%)
  local copies, waits for them, and re-layouts  24.3 us (6%)
  Pallas kernels  11 us (3%)
    ppermute x28, waiting for transfers between devices, rotated(): lax.ppermute(value, 'tensor', [(i, (i + steps) % count) for i in range(co...  230 us
    ppermute x28, starting transfers between devices, rotated(): lax.ppermute(value, 'tensor', [(i, (i + steps) % count) for i in range(co...  32.1 us
    ppermute x5, waiting for transfers between devices, shifted(): lax.ppermute(value, axis, [(source, source + steps) for source in range(i...  31.9 us
    dot_general x21, matrix products, dot_t(): lax.dot_general(left, right, (((1,), (1,)), ((), ())), preferred_element_...  27.6 us
    dot_general x22, matrix products, dot(): return jnp.dot(left, right, preferred_element_type=f32)  23.1 us
    unnamed x120, local copies, waits for them, and re-layouts  22.2 us
    ppermute x5, starting transfers between devices, shifted(): lax.ppermute(value, axis, [(source, source + steps) for source in range(i...  14.6 us
  transfers between devices with their start and end apart: 33, of which 21 were waited for; matrix products, arithmetic and copies ran while one was open for 18% of the time, Pallas kernels for 2%

commit v1 on v0

--- a/solution.py
+++ b/solution.py
@@ -75,17 +75,27 @@
     return lax.optimization_barrier((*values, *after))[: len(values)]
 
 
+def handed(value, steps):
+    sections, count = lax.axis_size("section"), lax.axis_size("tensor")
+    pairs = [
+        (s * count + t, (s + 1) % sections * count + (t + steps) % count)
+        for s in range(sections)
+        for t in range(count)
+    ]
+    return lax.ppermute(value, ("section", "tensor"), pairs)
+
+
 class Lane:
     def __init__(self, depth):
         self.depth = depth
         self.past = []
 
-    def send(self, value, steps, after=(), depth=None):
+    def send(self, value, steps, after=(), depth=None, move=rotated):
         depth = depth or self.depth
         if len(self.past) >= depth:
             after = (self.past[-depth], *after)
         value = fenced(value, after)
-        arrived = rotated(value, steps)
+        arrived = move(value, steps)
         self.past.append(arrived)
         return arrived
 
@@ -367,9 +377,10 @@
             + inverse[:, None] * (gain_cols * norm_grad - unit * along[:, None])
         ).astype(bf16)
 
-    def send_out(activated, downs, j, ahead=()):
+    def send_out(activated, downs, j):
         values = [dot(activated, piece(downs[k], j)).astype(bf16) for k in others]
-        return [lane.send(value, k, ahead) for value, k in zip(values, others)]
+        depth = 3 if j < 2 else 2
+        return [lane.send(value, k, depth=depth, move=handed) for value, k in zip(values, others)]
 
     def add_out(values, mine, terms):
         return (values.astype(f32) + total([mine] + [t.astype(f32) for t in terms])).astype(bf16)
@@ -417,12 +428,12 @@
     entering_pre = total([mine] + [t.astype(f32) for t in got]) * inverses[1][:, None]
 
     activated = jax.nn.silu(entering_pre).astype(bf16)
-    gots = [send_out(activated, last_downs, j) for j in pieces[:-1]]
-    mine = dot(activated, last_downs[0])
-    gots.append(send_out(activated, last_downs, final, [mine]))
+    mine = handed((entering.astype(f32) + dot(activated, last_downs[0])).astype(bf16), 0)
+    gots = [send_out(activated, last_downs, j) for j in pieces]
     first_got.append(send_up(first_parts[2], depth=3))
-    hidden = add_out(entering, mine, [jnp.concatenate(t, axis=1) for t in zip(*gots)])
-    entry = jnp.where(opening, section_entry, shifted(hidden, "section", 1))
+    incoming = [jnp.concatenate(t, axis=1).astype(f32) for t in zip(*gots)]
+    incoming = total([mine.astype(f32)] + incoming).astype(bf16)
+    entry = jnp.where(opening, section_entry, incoming)
 
     row_count, row_length = keep_mask.shape
     token_weights = jnp.concatenate(
@@ -440,8 +451,8 @@
         values = token_weights[:, :, None] * rows.astype(f32)[:, None, :]
         return values.reshape(tokens, rows.shape[1])
 
-    pooled = pool(fenced(hidden, [entry]))
-    pooled = [pooled] + [rotated(pooled, k) for k in others]
+    back = lax.axis_size("section") - 1
+    pooled = lax.ppermute(pool(fenced(incoming, [entry])), "section", [(0, back)])
 
     entry_squares = sum_small(square_sum(entry)[None, :])
     entry_inverse = settled(lax.rsqrt(entry_squares / full_width + epsilon))
@@ -449,6 +460,8 @@
     sent = other_products(pair, first_got, [entry_inverse])
     mine = dot(fenced(pair, sent), first_up_own)
     got = collect(sent)
+    pooled = fenced(pooled, sent)
+    pooled = [pooled] + [rotated(pooled, k) for k in others]
 
     pre_grad, along, entry_activated = gated(mine, got, [inverse_rows[0], entry_inverse], act_grad)
     first_blocks, first_along = exchange_grad(pre_grad, along)

time: 426 us -> 429 us (level)
  starting transfers between devices: 46.7 us -> 55.5 us
  waiting for transfers between devices: 262 us -> 255 us
    ppermute x0 -> x6, waiting for transfers between devices: none -> 43.8 us  [the longest x5 43.8 us: handed(): return lax.ppermute(value, ('section', 'tensor'), pairs)]
    ppermute x5 -> x4, waiting for transfers between devices: 31.9 us -> 0.02 us  [shifted(): lax.ppermute(value, axis, [(source, source + steps) for source in range(i...]
    ppermute x28 -> x24, waiting for transfers between devices: 230 us -> 211 us  [rotated(): lax.ppermute(value, 'tensor', [(i, (i + steps) % count) for i in range(co...]
    ppermute x0 -> x6, starting transfers between devices: none -> 6.03 us  [the longest x5 5.24 us: handed(): return lax.ppermute(value, ('section', 'tensor'), pairs)]
    ppermute x5 -> x4, starting transfers between devices: 14.6 us -> 20.6 us  [shifted(): lax.ppermute(value, axis, [(source, source + steps) for source in range(i...]
    ppermute x28 -> x24, starting transfers between devices: 32.1 us -> 28.8 us  [rotated(): lax.ppermute(value, 'tensor', [(i, (i + steps) % count) for i in range(co...]
    unnamed x120 -> x118, local copies, waits for them, and re-layouts: 22.2 us -> 24 us
  transfers between devices with their start and end apart: 33 -> 34, of which waited for: 21 -> 19; matrix products, arithmetic and copies ran while one was open for 18% -> 18% of each run, Pallas kernels for 2% -> 2%
where the time goes in v1:
time: 429 us; the launch traced here: 423 us
  waiting for transfers between devices  255 us (59%)
  starting transfers between devices  55.5 us (13%)
  matrix products  51.6 us (12%)
  local copies, waits for them, and re-layouts  26 us (6%)
  other arithmetic  22.2 us (5%)
  Pallas kernels  10.9 us (3%)
    ppermute x24, waiting for transfers between devices, rotated(): lax.ppermute(value, 'tensor', [(i, (i + steps) % count) for i in range(co...  211 us
    ppermute x5, waiting for transfers between devices, handed(): return lax.ppermute(value, ('section', 'tensor'), pairs)  43.8 us
    ppermute x24, starting transfers between devices, rotated(): lax.ppermute(value, 'tensor', [(i, (i + steps) % count) for i in range(co...  28.8 us
    dot_general x21, matrix products, dot_t(): lax.dot_general(left, right, (((1,), (1,)), ((), ())), preferred_element_...  27.5 us
    dot_general x22, matrix products, dot(): return jnp.dot(left, right, preferred_element_type=f32)  24.1 us
    unnamed x118, local copies, waits for them, and re-layouts  24 us
    ppermute x4, starting transfers between devices, shifted(): lax.ppermute(value, axis, [(source, source + steps) for source in range(i...  20.6 us
  transfers between devices with their start and end apart: 34, of which 19 were waited for; matrix products, arithmetic and copies ran while one was open for 18% of the time, Pallas kernels for 2%

profile of v1, /device:TPU:16, one launch (start us, length us, event | category | flops | bytes accessed | tf_op | source)
XLA Modules:
  0.0 423.3 jit_solution(13999888072699989065)
XLA Ops:
  11.4 5.0 %fusion.8 = (f32[256]{0:T(256)S(1)}, bf16[1,256,4096]{2,1,0:T(8,128)(2,1)}, f32[256]{0:T(256)S(1)}, bf16[256,4096]{1,0:T(8,128)(2,1)S(1)}) fusion(bf16[1,256,4096]{2,1,0:T(8,128)(2,1)} %param.17, bf16[1,256,4096]{2,1,0:T(8,128)(2,1)} %param.18, pred[]{:T(512)S(6)} %eq.21, f32[4096]{0:T(1024)S(1)} %bitcast.129), kind=kLoop, calls=%fused_computation.25 | loop fusion | flops 9436672 | bytes 8407041 | tf_op jit(solution)/shard_map/reduce_sum | solution.py:306
  18.9 3.4 copy-done.6
  30.6 4.1 copy-done.8
  38.3 11.2 %collective-permute-done.1 = bf16[256,4096]{1,0:T(8,128)(2,1)} collective-permute-done((bf16[256,4096]{1,0:T(8,128)(2,1)}, bf16[256,4096]{1,0:T(8,128)(2,1)}, u32[]{:S(2)}, u32[]{:S(2)}) %collective-permute-start.1) | collective-permute-done | bytes 2097184 | tf_op jit(solution)/shard_map/ppermute | solution.py:27
  52.9 41.6 %collective-permute-done = bf16[2048,512]{1,0:T(8,128)(2,1)} collective-permute-done((bf16[2048,512]{1,0:T(8,128)(2,1)}, bf16[2048,512]{1,0:T(8,128)(2,1)}, u32[]{:S(2)}, u32[]{:S(2)}) %collective-permute-start) | collective-permute-done | bytes 2097184 | tf_op jit(solution)/shard_map/ppermute | solution.py:27
  101.3 38.0 %collective-permute-done.2 = bf16[2048,512]{1,0:T(8,128)(2,1)S(1)} collective-permute-done((bf16[2048,512]{1,0:T(8,128)(2,1)S(1)}, bf16[2048,512]{1,0:T(8,128)(2,1)S(1)}, u32[]{:S(2)}, u32[]{:S(2)}) %collective-permute-start.2) | collective-permute-done | bytes 2097184 | tf_op jit(solution)/shard_map/ppermute | solution.py:27
  148.6 13.2 %collective-permute-done.8 = bf16[1024,512]{1,0:T(8,128)(2,1)S(1)} collective-permute-done((bf16[1024,512]{1,0:T(8,128)(2,1)S(1)}, bf16[1024,512]{1,0:T(8,128)(2,1)S(1)}, u32[]{:S(2)}, u32[]{:S(2)}) %collective-permute-start.8) | collective-permute-done | bytes 1048608 | tf_op jit(solution)/shard_map/ppermute | solution.py:27
  163.3 3.9 pad_maximum_fusion.1
  175.8 14.5 %collective-permute-done.9 = bf16[1024,512]{1,0:T(8,128)(2,1)S(1)} collective-permute-done((bf16[1024,512]{1,0:T(8,128)(2,1)S(1)}, bf16[1024,512]{1,0:T(8,128)(2,1)S(1)}, u32[]{:S(2)}, u32[]{:S(2)}) %collective-permute-start.9) | collective-permute-done | bytes 1048608 | tf_op jit(solution)/shard_map/ppermute | solution.py:27
  193.0 12.1 %collective-permute-done.7 = bf16[256,1024]{1,0:T(8,128)(2,1)S(1)} collective-permute-done((bf16[256,1024]{1,0:T(8,128)(2,1)S(1)}, bf16[256,1024]{1,0:T(8,128)(2,1)S(1)}, u32[]{:S(2)}, u32[]{:S(2)}) %collective-permute-start.7) | collective-permute-done | bytes 524320 | tf_op jit(solution)/shard_map/ppermute | solution.py:85
  205.8 11.5 %collective-permute-done.10 = bf16[256,1024]{1,0:T(8,128)(2,1)} collective-permute-done((bf16[256,1024]{1,0:T(8,128)(2,1)S(1)}, bf16[256,1024]{1,0:T(8,128)(2,1)}, u32[]{:S(2)}, u32[]{:S(2)}) %collective-permute-start.10) | collective-permute-done | bytes 524320 | tf_op jit(solution)/shard_map/ppermute | solution.py:85
  222.1 9.0 %collective-permute-done.11 = bf16[256,1024]{1,0:T(8,128)(2,1)} collective-permute-done((bf16[256,1024]{1,0:T(8,128)(2,1)}, bf16[256,1024]{1,0:T(8,128)(2,1)}, u32[]{:S(2)}, u32[]{:S(2)}) %collective-permute-start.11) | collective-permute-done | bytes 524320 | tf_op jit(solution)/shard_map/ppermute | solution.py:85
  231.1 11.2 %collective-permute-done.12 = bf16[256,1024]{1,0:T(8,128)(2,1)} collective-permute-done((bf16[256,1024]{1,0:T(8,128)(2,1)}, bf16[256,1024]{1,0:T(8,128)(2,1)}, u32[]{:S(2)}, u32[]{:S(2)}) %collective-permute-start.12) | collective-permute-done | bytes 524320 | tf_op jit(solution)/shard_map/ppermute | solution.py:85
  250.2 38.5 %collective-permute-done.13 = f32[1,256]{1,0:T(1,128)S(1)} collective-permute-done((f32[1,256]{1,0:T(1,128)S(1)}, f32[1,256]{1,0:T(1,128)S(1)}, u32[]{:S(2)}, u32[]{:S(2)}) %collective-permute-start.13) | collective-permute-done | bytes 1056 | tf_op jit(solution)/shard_map/ppermute | solution.py:27
  294.9 9.7 %collective-permute-done.15.refs_0_ = bf16[512,512]{1,0:T(8,128)(2,1)S(1)} collective-permute-done((bf16[512,512]{1,0:T(8,128)(2,1)S(1)}, bf16[512,512]{1,0:T(8,128)(2,1)S(1)}, u32[]{:S(2)}, u32[]{:S(2)}) %collective-permute-start.15) | collective-permute-done | bytes 524320 | tf_op jit(solution)/shard_map/ppermute | solution.py:27
  310.9 5.7 %collective-permute-done.16 = bf16[256,512]{1,0:T(8,128)(2,1)S(1)} collective-permute-done((bf16[256,512]{1,0:T(8,128)(2,1)S(1)}, bf16[256,512]{1,0:T(8,128)(2,1)S(1)}, u32[]{:S(2)}, u32[]{:S(2)}) %collective-permute-start.16) | collective-permute-done | bytes 262176 | tf_op jit(solution)/shard_map/ppermute | solution.py:27
  320.7 4.3 %collective-permute-start.21 = (bf16[256,1024]{1,0:T(8,128)(2,1)S(1)}, bf16[256,1024]{1,0:T(8,128)(2,1)}, u32[]{:S(2)}, u32[]{:S(2)}) collective-permute-start(bf16[256,1024]{1,0:T(8,128)(2,1)S(1)} %fusion.36), channel_id=1, source_target_pairs={{2,0},{4,2},{6,4},{8,6},{10,8},{12,10},{14,12},{16,14},{18,16},{20... | collective-permute-start | bytes 1572872 | tf_op jit(solution)/shard_map/ppermute | solution.py:22
  326.1 12.5 %collective-permute-start.25 = (bf16[256,1024]{1,0:T(8,128)(2,1)S(1)}, bf16[256,1024]{1,0:T(8,128)(2,1)}, u32[]{:S(2)}, u32[]{:S(2)}) collective-permute-start(bf16[256,1024]{1,0:T(8,128)(2,1)S(1)} %fusion.37), channel_id=1, source_target_pairs={{2,0},{4,2},{6,4},{8,6},{10,8},{12,10},{14,12},{16,14},{18,16},{20... | collective-permute-start | bytes 1572872 | tf_op jit(solution)/shard_map/ppermute | solution.py:22
  347.9 6.4 %collective-permute-done.28.refs_1_ = f32[1,4096]{1,0:T(1,128)S(1)} collective-permute-done((f32[1,4096]{1,0:T(1,128)S(1)}, f32[1,4096]{1,0:T(1,128)S(1)}, u32[]{:S(2)}, u32[]{:S(2)}) %collective-permute-start.28) | collective-permute-done | bytes 16416 | tf_op jit(solution)/shard_map/ppermute | solution.py:27
  360.5 3.7 fusion.86
  381.6 6.0 %collective-permute-done.23 = bf16[256,1024]{1,0:T(8,128)(2,1)S(1)} collective-permute-done((bf16[256,1024]{1,0:T(8,128)(2,1)S(1)}, bf16[256,1024]{1,0:T(8,128)(2,1)S(1)}, u32[]{:S(2)}, u32[]{:S(2)}) %collective-permute-start.23) | collective-permute-done | bytes 524320 | tf_op jit(solution)/shard_map/ppermute | solution.py:27
  389.2 12.2 %collective-permute-done.29.refs_1_ = bf16[256,1024]{1,0:T(8,128)(2,1)S(1)} collective-permute-done((bf16[256,1024]{1,0:T(8,128)(2,1)}, bf16[256,1024]{1,0:T(8,128)(2,1)S(1)}, u32[]{:S(2)}, u32[]{:S(2)}) %collective-permute-start.29) | collective-permute-done | bytes 524320 | tf_op jit(solution)/shard_map/ppermute | solution.py:27
  407.0 5.8 %collective-permute-done.32 = bf16[256,512]{1,0:T(8,128)(2,1)S(1)} collective-permute-done((bf16[256,512]{1,0:T(8,128)(2,1)S(1)}, bf16[256,512]{1,0:T(8,128)(2,1)S(1)}, u32[]{:S(2)}, u32[]{:S(2)}) %collective-permute-start.32) | collective-permute-done | bytes 262176 | tf_op jit(solution)/shard_map/ppermute | solution.py:27
  417.2 4.4 %collective-permute-done.30 = bf16[256,1024]{1,0:T(8,128)(2,1)S(1)} collective-permute-done((bf16[256,1024]{1,0:T(8,128)(2,1)S(1)}, bf16[256,1024]{1,0:T(8,128)(2,1)S(1)}, u32[]{:S(2)}, u32[]{:S(2)}) %collective-permute-start.30) | collective-permute-done | bytes 524320 | tf_op jit(solution)/shard_map/ppermute | solution.py:27
  (243 shorter events, 132.9 us)
Async XLA Ops:
  0.6 48.9 %collective-permute-start.1 = (bf16[256,4096]{1,0:T(8,128)(2,1)}, bf16[256,4096]{1,0:T(8,128)(2,1)}, u32[]{:S(2)}, u32[]{:S(2)}) collective-permute-start(bf16[256,4096]{1,0:T(8,128)(2,1)} %bitcast.156), channel_id=1, source_target_pairs={{0,1},{1,0},{2,3},{3,2},{4,5},{5,4},{6,7},{7,6},{8,9},{9,8},{10,11... | collective-permute-start | bytes 6291464 | tf_op jit(solution)/shard_map/ppermute | solution.py:27
  10.9 83.6 %collective-permute-start = (bf16[2048,512]{1,0:T(8,128)(2,1)}, bf16[2048,512]{1,0:T(8,128)(2,1)}, u32[]{:S(2)}, u32[]{:S(2)}) collective-permute-start(bf16[2048,512]{1,0:T(8,128)(2,1)} %get-tuple-element.63), channel_id=1, source_target_pairs={{0,1},{1,0},{2,3},{3,2},{4,5},{5,4},{6,7},{7,6},{8,9},{9,8},{10,11... | collective-permute-start | bytes 6291464 | tf_op jit(solution)/shard_map/ppermute | solution.py:27
  49.5 89.8 %collective-permute-start.2 = (bf16[2048,512]{1,0:T(8,128)(2,1)S(1)}, bf16[2048,512]{1,0:T(8,128)(2,1)S(1)}, u32[]{:S(2)}, u32[]{:S(2)}) collective-permute-start(bf16[2048,512]{1,0:T(8,128)(2,1)S(1)} %copy-done.26), channel_id=1, source_target_pairs={{0,1},{1,0},{2,3},{3,2},{4,5},{5,4},{6,7},{7,6},{8,9},{9,8},{10,11... | collective-permute-start | bytes 6291464 | tf_op jit(solution)/shard_map/ppermute | solution.py:27
  96.8 65.0 %collective-permute-start.8 = (bf16[1024,512]{1,0:T(8,128)(2,1)S(1)}, bf16[1024,512]{1,0:T(8,128)(2,1)S(1)}, u32[]{:S(2)}, u32[]{:S(2)}) collective-permute-start(bf16[1024,512]{1,0:T(8,128)(2,1)S(1)} %get-tuple-element.83), channel_id=1, source_target_pairs={{0,1},{1,0},{2,3},{3,2},{4,5},{5,4},{6,7},{7,6},{8,9},{9,8},{10,11... | collective-permute-start | bytes 3145736 | tf_op jit(solution)/shard_map/ppermute | solution.py:27
  142.4 26.3 %collective-permute-start.4 = (f32[3,256]{1,0:T(4,128)S(1)}, f32[3,256]{1,0:T(4,128)S(1)}, u32[]{:S(2)}, u32[]{:S(2)}) collective-permute-start(f32[3,256]{1,0:T(4,128)S(1)} %pad_maximum_fusion.3), channel_id=1, source_target_pairs={{0,1},{1,0},{2,3},{3,2},{4,5},{5,4},{6,7},{7,6},{8,9},{9,8},{10,11... | collective-permute-start | bytes 9224 | tf_op jit(solution)/shard_map/ppermute | solution.py:27
  143.9 25.0 %collective-permute-start.3 = (bf16[256,512]{1,0:T(8,128)(2,1)S(1)}, bf16[256,512]{1,0:T(8,128)(2,1)S(1)}, u32[]{:S(2)}, u32[]{:S(2)}) collective-permute-start(bf16[256,512]{1,0:T(8,128)(2,1)S(1)} %fusion.44), channel_id=1, source_target_pairs={{0,1},{1,0},{2,3},{3,2},{4,5},{5,4},{6,7},{7,6},{8,9},{9,8},{10,11... | collective-permute-start | bytes 786440 | tf_op jit(solution)/shard_map/ppermute | solution.py:27
  144.4 24.5 %collective-permute-start.5 = (f32[4,4096]{1,0:T(4,128)S(1)}, f32[4,4096]{1,0:T(4,128)S(1)}, u32[]{:S(2)}, u32[]{:S(2)}) collective-permute-start(f32[4,4096]{1,0:T(4,128)S(1)} %bitcast.135), channel_id=1, source_target_pairs={{0,1},{1,0},{2,3},{3,2},{4,5},{5,4},{6,7},{7,6},{8,9},{9,8},{10,11... | collective-permute-start | bytes 196616 | tf_op jit(solution)/shard_map/ppermute | solution.py:27
  161.8 28.4 %collective-permute-start.9 = (bf16[1024,512]{1,0:T(8,128)(2,1)S(1)}, bf16[1024,512]{1,0:T(8,128)(2,1)S(1)}, u32[]{:S(2)}, u32[]{:S(2)}) collective-permute-start(bf16[1024,512]{1,0:T(8,128)(2,1)S(1)} %get-tuple-element.84), channel_id=1, source_target_pairs={{0,1},{1,0},{2,3},{3,2},{4,5},{5,4},{6,7},{7,6},{8,9},{9,8},{10,11... | collective-permute-start | bytes 3145736 | tf_op jit(solution)/shard_map/ppermute | solution.py:27
  171.8 70.6 %collective-permute-start.6 = (bf16[256,4096]{1,0:T(8,128)(2,1)}, bf16[256,4096]{1,0:T(8,128)(2,1)}, u32[]{:S(2)}, u32[]{:S(2)}) collective-permute-start(bf16[256,4096]{1,0:T(8,128)(2,1)} %fusion), channel_id=1, source_target_pairs={{0,2},{1,3},{2,4},{3,5},{4,6},{5,7},{6,8},{7,9},{8,10},{9,11},{10,... | collective-permute-start | bytes 6291464 | tf_op jit(solution)/shard_map/ppermute | solution.py:85
  172.3 32.8 %collective-permute-start.7 = (bf16[256,1024]{1,0:T(8,128)(2,1)S(1)}, bf16[256,1024]{1,0:T(8,128)(2,1)S(1)}, u32[]{:S(2)}, u32[]{:S(2)}) collective-permute-start(bf16[256,1024]{1,0:T(8,128)(2,1)S(1)} %convolution_convert_fusion.6), channel_id=1, source_target_pairs={{0,3},{1,2},{2,5},{3,4},{4,7},{5,6},{6,9},{7,8},{8,11},{9,10},{10,... | collective-permute-start | bytes 1572872 | tf_op jit(solution)/shard_map/ppermute | solution.py:85
  190.2 27.1 %collective-permute-start.10 = (bf16[256,1024]{1,0:T(8,128)(2,1)S(1)}, bf16[256,1024]{1,0:T(8,128)(2,1)}, u32[]{:S(2)}, u32[]{:S(2)}) collective-permute-start(bf16[256,1024]{1,0:T(8,128)(2,1)S(1)} %convolution_convert_fusion.5), channel_id=1, source_target_pairs={{0,3},{1,2},{2,5},{3,4},{4,7},{5,6},{6,9},{7,8},{8,11},{9,10},{10,... | collective-permute-start | bytes 1572872 | tf_op jit(solution)/shard_map/ppermute | solution.py:85
  205.8 25.3 %collective-permute-start.11 = (bf16[256,1024]{1,0:T(8,128)(2,1)}, bf16[256,1024]{1,0:T(8,128)(2,1)}, u32[]{:S(2)}, u32[]{:S(2)}) collective-permute-start(bf16[256,1024]{1,0:T(8,128)(2,1)} %convolution_convert_fusion.4), channel_id=1, source_target_pairs={{0,3},{1,2},{2,5},{3,4},{4,7},{5,6},{6,9},{7,8},{8,11},{9,10},{10,... | collective-permute-start | bytes 1572872 | tf_op jit(solution)/shard_map/ppermute | solution.py:85
  217.4 25.0 %collective-permute-start.12 = (bf16[256,1024]{1,0:T(8,128)(2,1)}, bf16[256,1024]{1,0:T(8,128)(2,1)}, u32[]{:S(2)}, u32[]{:S(2)}) collective-permute-start(bf16[256,1024]{1,0:T(8,128)(2,1)} %convolution_convert_fusion.3), channel_id=1, source_target_pairs={{0,3},{1,2},{2,5},{3,4},{4,7},{5,6},{6,9},{7,8},{8,11},{9,10},{10,... | collective-permute-start | bytes 1572872 | tf_op jit(solution)/shard_map/ppermute | solution.py:85
  220.0 169.1 %collective-permute-start.31 = (bf16[256,512]{1,0:T(8,128)(2,1)}, bf16[256,512]{1,0:T(8,128)(2,1)S(1)}, u32[]{:S(2)}, u32[]{:S(2)}) collective-permute-start(bf16[256,512]{1,0:T(8,128)(2,1)} %fusion.45), channel_id=1, source_target_pairs={{0,1},{1,0},{2,3},{3,2},{4,5},{5,4},{6,7},{7,6},{8,9},{9,8},{10,11... | collective-permute-start | bytes 786440 | tf_op jit(solution)/shard_map/ppermute | solution.py:27
  220.6 68.2 %collective-permute-start.14 = (bf16[2048,512]{1,0:T(8,128)(2,1)}, bf16[2048,512]{1,0:T(8,128)(2,1)S(1)}, u32[]{:S(2)}, u32[]{:S(2)}) collective-permute-start(bf16[2048,512]{1,0:T(8,128)(2,1)} %copy-done.24), channel_id=1, source_target_pairs={{0,1},{1,0},{2,3},{3,2},{4,5},{5,4},{6,7},{7,6},{8,9},{9,8},{10,11... | collective-permute-start | bytes 6291464 | tf_op jit(solution)/shard_map/ppermute | solution.py:27
  247.1 42.9 %collective-permute-start.27 = (f32[1,4096]{1,0:T(1,128)S(1)}, f32[1,4096]{1,0:T(1,128)S(1)}, u32[]{:S(2)}, u32[]{:S(2)}) collective-permute-start(f32[1,4096]{1,0:T(1,128)S(1)} %fusion.92), channel_id=1, source_target_pairs={{0,30},{1,31}} | collective-permute-start | bytes 49160 | tf_op jit(solution)/shard_map/ppermute | solution.py:455
  247.9 40.9 %collective-permute-start.13 = (f32[1,256]{1,0:T(1,128)S(1)}, f32[1,256]{1,0:T(1,128)S(1)}, u32[]{:S(2)}, u32[]{:S(2)}) collective-permute-start(f32[1,256]{1,0:T(1,128)S(1)} %bitcast.143), channel_id=1, source_target_pairs={{0,1},{1,0},{2,3},{3,2},{4,5},{5,4},{6,7},{7,6},{8,9},{9,8},{10,11... | collective-permute-start | bytes 3080 | tf_op jit(solution)/shard_map/ppermute | solution.py:27
  308.8 38.1 %collective-permute-start.20 = (bf16[256,2048]{1,0:T(8,128)(2,1)S(1)}, bf16[256,2048]{1,0:T(8,128)(2,1)S(1)}, u32[]{:S(2)}, u32[]{:S(2)}) collective-permute-start(bf16[256,2048]{1,0:T(8,128)(2,1)S(1)} %convolution_convert_fusion), channel_id=1, source_target_pairs={{0,1},{1,0},{2,3},{3,2},{4,5},{5,4},{6,7},{7,6},{8,9},{9,8},{10,11... | collective-permute-start | bytes 3145736 | tf_op jit(solution)/shard_map/ppermute | solution.py:27
  317.7 21.4 %collective-permute-start.18 = (bf16[256,1024]{1,0:T(8,128)(2,1)S(1)}, bf16[256,1024]{1,0:T(8,128)(2,1)S(1)}, u32[]{:S(2)}, u32[]{:S(2)}) collective-permute-start(bf16[256,1024]{1,0:T(8,128)(2,1)S(1)} %fusion.35), channel_id=1, source_target_pairs={{2,0},{4,2},{6,4},{8,6},{10,8},{12,10},{14,12},{16,14},{18,16},{20... | collective-permute-start | bytes 1572872 | tf_op jit(solution)/shard_map/ppermute | solution.py:22
  320.7 24.2 %collective-permute-start.21 = (bf16[256,1024]{1,0:T(8,128)(2,1)S(1)}, bf16[256,1024]{1,0:T(8,128)(2,1)}, u32[]{:S(2)}, u32[]{:S(2)}) collective-permute-start(bf16[256,1024]{1,0:T(8,128)(2,1)S(1)} %fusion.36), channel_id=1, source_target_pairs={{2,0},{4,2},{6,4},{8,6},{10,8},{12,10},{14,12},{16,14},{18,16},{20... | collective-permute-start | bytes 1572872 | tf_op jit(solution)/shard_map/ppermute | solution.py:22
  345.0 20.6 %collective-permute-start.24 = (bf16[256,1024]{1,0:T(8,128)(2,1)}, bf16[256,1024]{1,0:T(8,128)(2,1)}, u32[]{:S(2)}, u32[]{:S(2)}) collective-permute-start(bf16[256,1024]{1,0:T(8,128)(2,1)} %fusion.38), channel_id=1, source_target_pairs={{2,0},{4,2},{6,4},{8,6},{10,8},{12,10},{14,12},{16,14},{18,16},{20... | collective-permute-start | bytes 1572872 | tf_op jit(solution)/shard_map/ppermute | solution.py:22
  346.9 23.9 %collective-permute-start.22 = (bf16[256,1024]{1,0:T(8,128)(2,1)}, bf16[256,1024]{1,0:T(8,128)(2,1)}, u32[]{:S(2)}, u32[]{:S(2)}) collective-permute-start(bf16[256,1024]{1,0:T(8,128)(2,1)} %collective-permute-done.21), channel_id=1, source_target_pairs={{0,1},{1,0},{2,3},{3,2},{4,5},{5,4},{6,7},{7,6},{8,9},{9,8},{10,11... | collective-permute-start | bytes 1572872 | tf_op jit(solution)/shard_map/ppermute | solution.py:27
  356.5 20.3 %collective-permute-start.26 = (bf16[256,1024]{1,0:T(8,128)(2,1)}, bf16[256,1024]{1,0:T(8,128)(2,1)}, u32[]{:S(2)}, u32[]{:S(2)}) collective-permute-start(bf16[256,1024]{1,0:T(8,128)(2,1)} %collective-permute-done.25), channel_id=1, source_target_pairs={{0,1},{1,0},{2,3},{3,2},{4,5},{5,4},{6,7},{7,6},{8,9},{9,8},{10,11... | collective-permute-start | bytes 1572872 | tf_op jit(solution)/shard_map/ppermute | solution.py:27
  370.8 16.8 %collective-permute-start.23 = (bf16[256,1024]{1,0:T(8,128)(2,1)S(1)}, bf16[256,1024]{1,0:T(8,128)(2,1)S(1)}, u32[]{:S(2)}, u32[]{:S(2)}) collective-permute-start(bf16[256,1024]{1,0:T(8,128)(2,1)S(1)} %convolution_convert_fusion.2), channel_id=1, source_target_pairs={{0,1},{1,0},{2,3},{3,2},{4,5},{5,4},{6,7},{7,6},{8,9},{9,8},{10,11... | collective-permute-start | bytes 1572872 | tf_op jit(solution)/shard_map/ppermute | solution.py:27
  (70 other events, 1167.9 us)

commit v2 on v0

--- a/solution.py
+++ b/solution.py
@@ -369,7 +369,8 @@
 
     def send_out(activated, downs, j, ahead=()):
         values = [dot(activated, piece(downs[k], j)).astype(bf16) for k in others]
-        return [lane.send(value, k, ahead) for value, k in zip(values, others)]
+        depth = 3 if j < 2 else 2
+        return [lane.send(value, k, ahead, depth) for value, k in zip(values, others)]
 
     def add_out(values, mine, terms):
         return (values.astype(f32) + total([mine] + [t.astype(f32) for t in terms])).astype(bf16)
@@ -441,7 +442,6 @@
         return values.reshape(tokens, rows.shape[1])
 
     pooled = pool(fenced(hidden, [entry]))
-    pooled = [pooled] + [rotated(pooled, k) for k in others]
 
     entry_squares = sum_small(square_sum(entry)[None, :])
     entry_inverse = settled(lax.rsqrt(entry_squares / full_width + epsilon))
@@ -449,6 +449,8 @@
     sent = other_products(pair, first_got, [entry_inverse])
     mine = dot(fenced(pair, sent), first_up_own)
     got = collect(sent)
+    pooled = fenced(pooled, sent)
+    pooled = [pooled] + [rotated(pooled, k) for k in others]
 
     pre_grad, along, entry_activated = gated(mine, got, [inverse_rows[0], entry_inverse], act_grad)
     first_blocks, first_along = exchange_grad(pre_grad, along)

time: 426 us -> 425 us (level)
  no operation moved by 1% of the time
where the time goes in v2:
time: 425 us; the launch traced here: 421 us
  waiting for transfers between devices  259 us (61%)
  matrix products  51.1 us (12%)
  starting transfers between devices  47.8 us (11%)
  local copies, waits for them, and re-layouts  24.6 us (6%)
  other arithmetic  24.4 us (6%)
  Pallas kernels  11 us (3%)
    ppermute x28, waiting for transfers between devices, rotated(): lax.ppermute(value, 'tensor', [(i, (i + steps) % count) for i in range(co...  228 us
    ppermute x28, starting transfers between devices, rotated(): lax.ppermute(value, 'tensor', [(i, (i + steps) % count) for i in range(co...  33.4 us
    ppermute x5, waiting for transfers between devices, shifted(): lax.ppermute(value, axis, [(source, source + steps) for source in range(i...  31.4 us
    dot_general x21, matrix products, dot_t(): lax.dot_general(left, right, (((1,), (1,)), ((), ())), preferred_element_...  27.5 us
    dot_general x22, matrix products, dot(): return jnp.dot(left, right, preferred_element_type=f32)  23.6 us
    unnamed x120, local copies, waits for them, and re-layouts  22.5 us
    ppermute x5, starting transfers between devices, shifted(): lax.ppermute(value, axis, [(source, source + steps) for source in range(i...  14.4 us
  transfers between devices with their start and end apart: 33, of which 21 were waited for; matrix products, arithmetic and copies ran while one was open for 18% of the time, Pallas kernels for 2%

profile of v2, /device:TPU:16, one launch (start us, length us, event | category | flops | bytes accessed | tf_op | source)
XLA Modules:
  0.0 420.8 jit_solution(12082303408659809444)
XLA Ops:
  11.4 5.0 %fusion.8 = (f32[256]{0:T(256)S(1)}, bf16[1,256,4096]{2,1,0:T(8,128)(2,1)}, f32[256]{0:T(256)S(1)}, bf16[256,4096]{1,0:T(8,128)(2,1)S(1)}) fusion(bf16[1,256,4096]{2,1,0:T(8,128)(2,1)} %param.17, bf16[1,256,4096]{2,1,0:T(8,128)(2,1)} %param.18, pred[]{:T(512)S(6)} %eq.21, f32[4096]{0:T(1024)S(1)} %bitcast.129), kind=kLoop, calls=%fused_computation.25 | loop fusion | flops 9436672 | bytes 8407041 | tf_op jit(solution)/shard_map/reduce_sum | solution.py:296
  30.5 4.1 copy-done.8
  38.3 11.3 %collective-permute-done.1 = bf16[256,4096]{1,0:T(8,128)(2,1)} collective-permute-done((bf16[256,4096]{1,0:T(8,128)(2,1)}, bf16[256,4096]{1,0:T(8,128)(2,1)}, u32[]{:S(2)}, u32[]{:S(2)}) %collective-permute-start.1) | collective-permute-done | bytes 2097184 | tf_op jit(solution)/shard_map/ppermute | solution.py:27
  52.9 41.6 %collective-permute-done = bf16[2048,512]{1,0:T(8,128)(2,1)} collective-permute-done((bf16[2048,512]{1,0:T(8,128)(2,1)}, bf16[2048,512]{1,0:T(8,128)(2,1)}, u32[]{:S(2)}, u32[]{:S(2)}) %collective-permute-start) | collective-permute-done | bytes 2097184 | tf_op jit(solution)/shard_map/ppermute | solution.py:27
  101.3 38.0 %collective-permute-done.2 = bf16[2048,512]{1,0:T(8,128)(2,1)S(1)} collective-permute-done((bf16[2048,512]{1,0:T(8,128)(2,1)S(1)}, bf16[2048,512]{1,0:T(8,128)(2,1)S(1)}, u32[]{:S(2)}, u32[]{:S(2)}) %collective-permute-start.2) | collective-permute-done | bytes 2097184 | tf_op jit(solution)/shard_map/ppermute | solution.py:27
  148.6 13.2 %collective-permute-done.7 = bf16[1024,512]{1,0:T(8,128)(2,1)S(1)} collective-permute-done((bf16[1024,512]{1,0:T(8,128)(2,1)S(1)}, bf16[1024,512]{1,0:T(8,128)(2,1)S(1)}, u32[]{:S(2)}, u32[]{:S(2)}) %collective-permute-start.7) | collective-permute-done | bytes 1048608 | tf_op jit(solution)/shard_map/ppermute | solution.py:27
  163.3 3.8 pad_maximum_fusion.1
  172.1 19.3 %collective-permute-done.8 = bf16[1024,512]{1,0:T(8,128)(2,1)S(1)} collective-permute-done((bf16[1024,512]{1,0:T(8,128)(2,1)S(1)}, bf16[1024,512]{1,0:T(8,128)(2,1)S(1)}, u32[]{:S(2)}, u32[]{:S(2)}) %collective-permute-start.8) | collective-permute-done | bytes 1048608 | tf_op jit(solution)/shard_map/ppermute | solution.py:27
  194.7 8.0 %collective-permute-done.6 = bf16[256,1024]{1,0:T(8,128)(2,1)S(1)} collective-permute-done((bf16[256,1024]{1,0:T(8,128)(2,1)S(1)}, bf16[256,1024]{1,0:T(8,128)(2,1)S(1)}, u32[]{:S(2)}, u32[]{:S(2)}) %collective-permute-start.6) | collective-permute-done | bytes 524320 | tf_op jit(solution)/shard_map/ppermute | solution.py:27
  204.1 9.7 %collective-permute-done.9 = bf16[256,1024]{1,0:T(8,128)(2,1)S(1)} collective-permute-done((bf16[256,1024]{1,0:T(8,128)(2,1)S(1)}, bf16[256,1024]{1,0:T(8,128)(2,1)S(1)}, u32[]{:S(2)}, u32[]{:S(2)}) %collective-permute-start.9) | collective-permute-done | bytes 524320 | tf_op jit(solution)/shard_map/ppermute | solution.py:27
  215.4 9.7 %collective-permute-done.10 = bf16[256,1024]{1,0:T(8,128)(2,1)S(1)} collective-permute-done((bf16[256,1024]{1,0:T(8,128)(2,1)S(1)}, bf16[256,1024]{1,0:T(8,128)(2,1)S(1)}, u32[]{:S(2)}, u32[]{:S(2)}) %collective-permute-start.10) | collective-permute-done | bytes 524320 | tf_op jit(solution)/shard_map/ppermute | solution.py:27
  225.1 10.1 %collective-permute-done.11 = bf16[256,1024]{1,0:T(8,128)(2,1)S(1)} collective-permute-done((bf16[256,1024]{1,0:T(8,128)(2,1)S(1)}, bf16[256,1024]{1,0:T(8,128)(2,1)S(1)}, u32[]{:S(2)}, u32[]{:S(2)}) %collective-permute-start.11) | collective-permute-done | bytes 524320 | tf_op jit(solution)/shard_map/ppermute | solution.py:27
  241.8 23.7 %collective-permute-done.12 = bf16[256,4096]{1,0:T(8,128)(2,1)} collective-permute-done((bf16[256,4096]{1,0:T(8,128)(2,1)}, bf16[256,4096]{1,0:T(8,128)(2,1)}, u32[]{:S(2)}, u32[]{:S(2)}) %collective-permute-start.12) | collective-permute-done | bytes 2097184 | tf_op jit(solution)/shard_map/ppermute | solution.py:22
  275.2 18.5 %collective-permute-done.13 = f32[1,256]{1,0:T(1,128)S(1)} collective-permute-done((f32[1,256]{1,0:T(1,128)S(1)}, f32[1,256]{1,0:T(1,128)S(1)}, u32[]{:S(2)}, u32[]{:S(2)}) %collective-permute-start.13) | collective-permute-done | bytes 1056 | tf_op jit(solution)/shard_map/ppermute | solution.py:27
  298.9 10.3 %collective-permute-done.15.refs_0_ = bf16[512,512]{1,0:T(8,128)(2,1)S(1)} collective-permute-done((bf16[512,512]{1,0:T(8,128)(2,1)S(1)}, bf16[512,512]{1,0:T(8,128)(2,1)S(1)}, u32[]{:S(2)}, u32[]{:S(2)}) %collective-permute-start.15) | collective-permute-done | bytes 524320 | tf_op jit(solution)/shard_map/ppermute | solution.py:27
  314.5 6.4 %collective-permute-done.16 = bf16[256,512]{1,0:T(8,128)(2,1)S(1)} collective-permute-done((bf16[256,512]{1,0:T(8,128)(2,1)S(1)}, bf16[256,512]{1,0:T(8,128)(2,1)S(1)}, u32[]{:S(2)}, u32[]{:S(2)}) %collective-permute-start.16) | collective-permute-done | bytes 262176 | tf_op jit(solution)/shard_map/ppermute | solution.py:27
  334.1 7.7 %collective-permute-done.25 = bf16[256,1024]{1,0:T(8,128)(2,1)} collective-permute-done((bf16[256,1024]{1,0:T(8,128)(2,1)S(1)}, bf16[256,1024]{1,0:T(8,128)(2,1)}, u32[]{:S(2)}, u32[]{:S(2)}) %collective-permute-start.25) | collective-permute-done | bytes 524320 | tf_op jit(solution)/shard_map/ppermute | solution.py:22
  344.8 4.8 %collective-permute-start.24 = (bf16[256,1024]{1,0:T(8,128)(2,1)}, bf16[256,1024]{1,0:T(8,128)(2,1)}, u32[]{:S(2)}, u32[]{:S(2)}) collective-permute-start(bf16[256,1024]{1,0:T(8,128)(2,1)} %fusion.38), channel_id=1, source_target_pairs={{2,0},{4,2},{6,4},{8,6},{10,8},{12,10},{14,12},{16,14},{18,16},{20... | collective-permute-start | bytes 1572872 | tf_op jit(solution)/shard_map/ppermute | solution.py:22
  351.1 3.7 collective-permute-done.27.refs_1_
  360.2 3.7 fusion.86
  382.1 4.8 %collective-permute-done.23 = bf16[256,1024]{1,0:T(8,128)(2,1)S(1)} collective-permute-done((bf16[256,1024]{1,0:T(8,128)(2,1)S(1)}, bf16[256,1024]{1,0:T(8,128)(2,1)S(1)}, u32[]{:S(2)}, u32[]{:S(2)}) %collective-permute-start.23) | collective-permute-done | bytes 524320 | tf_op jit(solution)/shard_map/ppermute | solution.py:27
  388.1 11.4 %collective-permute-done.28.refs_1_ = bf16[256,1024]{1,0:T(8,128)(2,1)S(1)} collective-permute-done((bf16[256,1024]{1,0:T(8,128)(2,1)}, bf16[256,1024]{1,0:T(8,128)(2,1)S(1)}, u32[]{:S(2)}, u32[]{:S(2)}) %collective-permute-start.28) | collective-permute-done | bytes 524320 | tf_op jit(solution)/shard_map/ppermute | solution.py:27
  405.1 5.8 %collective-permute-done.31 = bf16[256,512]{1,0:T(8,128)(2,1)S(1)} collective-permute-done((bf16[256,512]{1,0:T(8,128)(2,1)S(1)}, bf16[256,512]{1,0:T(8,128)(2,1)S(1)}, u32[]{:S(2)}, u32[]{:S(2)}) %collective-permute-start.31) | collective-permute-done | bytes 262176 | tf_op jit(solution)/shard_map/ppermute | solution.py:27
  415.3 3.5 collective-permute-done.29
  (244 shorter events, 140.1 us)
Async XLA Ops:
  0.6 48.9 %collective-permute-start.1 = (bf16[256,4096]{1,0:T(8,128)(2,1)}, bf16[256,4096]{1,0:T(8,128)(2,1)}, u32[]{:S(2)}, u32[]{:S(2)}) collective-permute-start(bf16[256,4096]{1,0:T(8,128)(2,1)} %bitcast.156), channel_id=1, source_target_pairs={{0,1},{1,0},{2,3},{3,2},{4,5},{5,4},{6,7},{7,6},{8,9},{9,8},{10,11... | collective-permute-start | bytes 6291464 | tf_op jit(solution)/shard_map/ppermute | solution.py:27
  10.9 83.6 %collective-permute-start = (bf16[2048,512]{1,0:T(8,128)(2,1)}, bf16[2048,512]{1,0:T(8,128)(2,1)}, u32[]{:S(2)}, u32[]{:S(2)}) collective-permute-start(bf16[2048,512]{1,0:T(8,128)(2,1)} %get-tuple-element.63), channel_id=1, source_target_pairs={{0,1},{1,0},{2,3},{3,2},{4,5},{5,4},{6,7},{7,6},{8,9},{9,8},{10,11... | collective-permute-start | bytes 6291464 | tf_op jit(solution)/shard_map/ppermute | solution.py:27
  49.5 89.8 %collective-permute-start.2 = (bf16[2048,512]{1,0:T(8,128)(2,1)S(1)}, bf16[2048,512]{1,0:T(8,128)(2,1)S(1)}, u32[]{:S(2)}, u32[]{:S(2)}) collective-permute-start(bf16[2048,512]{1,0:T(8,128)(2,1)S(1)} %copy-done.26), channel_id=1, source_target_pairs={{0,1},{1,0},{2,3},{3,2},{4,5},{5,4},{6,7},{7,6},{8,9},{9,8},{10,11... | collective-permute-start | bytes 6291464 | tf_op jit(solution)/shard_map/ppermute | solution.py:27
  96.8 65.0 %collective-permute-start.7 = (bf16[1024,512]{1,0:T(8,128)(2,1)S(1)}, bf16[1024,512]{1,0:T(8,128)(2,1)S(1)}, u32[]{:S(2)}, u32[]{:S(2)}) collective-permute-start(bf16[1024,512]{1,0:T(8,128)(2,1)S(1)} %get-tuple-element.83), channel_id=1, source_target_pairs={{0,1},{1,0},{2,3},{3,2},{4,5},{5,4},{6,7},{7,6},{8,9},{9,8},{10,11... | collective-permute-start | bytes 3145736 | tf_op jit(solution)/shard_map/ppermute | solution.py:27
  142.4 26.2 %collective-permute-start.4 = (f32[3,256]{1,0:T(4,128)S(1)}, f32[3,256]{1,0:T(4,128)S(1)}, u32[]{:S(2)}, u32[]{:S(2)}) collective-permute-start(f32[3,256]{1,0:T(4,128)S(1)} %pad_maximum_fusion.3), channel_id=1, source_target_pairs={{0,1},{1,0},{2,3},{3,2},{4,5},{5,4},{6,7},{7,6},{8,9},{9,8},{10,11... | collective-permute-start | bytes 9224 | tf_op jit(solution)/shard_map/ppermute | solution.py:27
  143.9 25.0 %collective-permute-start.3 = (bf16[256,512]{1,0:T(8,128)(2,1)S(1)}, bf16[256,512]{1,0:T(8,128)(2,1)S(1)}, u32[]{:S(2)}, u32[]{:S(2)}) collective-permute-start(bf16[256,512]{1,0:T(8,128)(2,1)S(1)} %fusion.44), channel_id=1, source_target_pairs={{0,1},{1,0},{2,3},{3,2},{4,5},{5,4},{6,7},{7,6},{8,9},{9,8},{10,11... | collective-permute-start | bytes 786440 | tf_op jit(solution)/shard_map/ppermute | solution.py:27
  144.5 24.5 %collective-permute-start.5 = (f32[4,4096]{1,0:T(4,128)S(1)}, f32[4,4096]{1,0:T(4,128)S(1)}, u32[]{:S(2)}, u32[]{:S(2)}) collective-permute-start(f32[4,4096]{1,0:T(4,128)S(1)} %bitcast.135), channel_id=1, source_target_pairs={{0,1},{1,0},{2,3},{3,2},{4,5},{5,4},{6,7},{7,6},{8,9},{9,8},{10,11... | collective-permute-start | bytes 196616 | tf_op jit(solution)/shard_map/ppermute | solution.py:27
  161.8 29.6 %collective-permute-start.8 = (bf16[1024,512]{1,0:T(8,128)(2,1)S(1)}, bf16[1024,512]{1,0:T(8,128)(2,1)S(1)}, u32[]{:S(2)}, u32[]{:S(2)}) collective-permute-start(bf16[1024,512]{1,0:T(8,128)(2,1)S(1)} %get-tuple-element.84), channel_id=1, source_target_pairs={{0,1},{1,0},{2,3},{3,2},{4,5},{5,4},{6,7},{7,6},{8,9},{9,8},{10,11... | collective-permute-start | bytes 3145736 | tf_op jit(solution)/shard_map/ppermute | solution.py:27
  169.9 32.7 %collective-permute-start.6 = (bf16[256,1024]{1,0:T(8,128)(2,1)S(1)}, bf16[256,1024]{1,0:T(8,128)(2,1)S(1)}, u32[]{:S(2)}, u32[]{:S(2)}) collective-permute-start(bf16[256,1024]{1,0:T(8,128)(2,1)S(1)} %convolution_convert_fusion.6), channel_id=1, source_target_pairs={{0,1},{1,0},{2,3},{3,2},{4,5},{5,4},{6,7},{7,6},{8,9},{9,8},{10,11... | collective-permute-start | bytes 1572872 | tf_op jit(solution)/shard_map/ppermute | solution.py:27
  191.4 22.5 %collective-permute-start.9 = (bf16[256,1024]{1,0:T(8,128)(2,1)S(1)}, bf16[256,1024]{1,0:T(8,128)(2,1)S(1)}, u32[]{:S(2)}, u32[]{:S(2)}) collective-permute-start(bf16[256,1024]{1,0:T(8,128)(2,1)S(1)} %convolution_convert_fusion.5), channel_id=1, source_target_pairs={{0,1},{1,0},{2,3},{3,2},{4,5},{5,4},{6,7},{7,6},{8,9},{9,8},{10,11... | collective-permute-start | bytes 1572872 | tf_op jit(solution)/shard_map/ppermute | solution.py:27
  202.6 22.5 %collective-permute-start.10 = (bf16[256,1024]{1,0:T(8,128)(2,1)S(1)}, bf16[256,1024]{1,0:T(8,128)(2,1)S(1)}, u32[]{:S(2)}, u32[]{:S(2)}) collective-permute-start(bf16[256,1024]{1,0:T(8,128)(2,1)S(1)} %convolution_convert_fusion.4), channel_id=1, source_target_pairs={{0,1},{1,0},{2,3},{3,2},{4,5},{5,4},{6,7},{7,6},{8,9},{9,8},{10,11... | collective-permute-start | bytes 1572872 | tf_op jit(solution)/shard_map/ppermute | solution.py:27
  213.8 21.3 %collective-permute-start.11 = (bf16[256,1024]{1,0:T(8,128)(2,1)S(1)}, bf16[256,1024]{1,0:T(8,128)(2,1)S(1)}, u32[]{:S(2)}, u32[]{:S(2)}) collective-permute-start(bf16[256,1024]{1,0:T(8,128)(2,1)S(1)} %convolution_convert_fusion.3), channel_id=1, source_target_pairs={{0,1},{1,0},{2,3},{3,2},{4,5},{5,4},{6,7},{7,6},{8,9},{9,8},{10,11... | collective-permute-start | bytes 1572872 | tf_op jit(solution)/shard_map/ppermute | solution.py:27
  236.9 28.6 %collective-permute-start.12 = (bf16[256,4096]{1,0:T(8,128)(2,1)}, bf16[256,4096]{1,0:T(8,128)(2,1)}, u32[]{:S(2)}, u32[]{:S(2)}) collective-permute-start(bf16[256,4096]{1,0:T(8,128)(2,1)} %fusion.6), channel_id=1, source_target_pairs={{0,2},{2,4},{4,6},{6,8},{8,10},{10,12},{12,14},{14,16},{16,18},{18... | collective-permute-start | bytes 6291464 | tf_op jit(solution)/shard_map/ppermute | solution.py:22
  239.8 148.3 %collective-permute-start.30 = (bf16[256,512]{1,0:T(8,128)(2,1)}, bf16[256,512]{1,0:T(8,128)(2,1)S(1)}, u32[]{:S(2)}, u32[]{:S(2)}) collective-permute-start(bf16[256,512]{1,0:T(8,128)(2,1)} %fusion.45), channel_id=1, source_target_pairs={{0,1},{1,0},{2,3},{3,2},{4,5},{5,4},{6,7},{7,6},{8,9},{9,8},{10,11... | collective-permute-start | bytes 786440 | tf_op jit(solution)/shard_map/ppermute | solution.py:27
  241.3 52.3 %collective-permute-start.14 = (bf16[2048,512]{1,0:T(8,128)(2,1)}, bf16[2048,512]{1,0:T(8,128)(2,1)S(1)}, u32[]{:S(2)}, u32[]{:S(2)}) collective-permute-start(bf16[2048,512]{1,0:T(8,128)(2,1)} %copy-done.24), channel_id=1, source_target_pairs={{0,1},{1,0},{2,3},{3,2},{4,5},{5,4},{6,7},{7,6},{8,9},{9,8},{10,11... | collective-permute-start | bytes 6291464 | tf_op jit(solution)/shard_map/ppermute | solution.py:27
  268.5 25.1 %collective-permute-start.13 = (f32[1,256]{1,0:T(1,128)S(1)}, f32[1,256]{1,0:T(1,128)S(1)}, u32[]{:S(2)}, u32[]{:S(2)}) collective-permute-start(f32[1,256]{1,0:T(1,128)S(1)} %bitcast.150), channel_id=1, source_target_pairs={{0,1},{1,0},{2,3},{3,2},{4,5},{5,4},{6,7},{7,6},{8,9},{9,8},{10,11... | collective-permute-start | bytes 3080 | tf_op jit(solution)/shard_map/ppermute | solution.py:27
  312.9 36.6 %collective-permute-start.20 = (bf16[256,2048]{1,0:T(8,128)(2,1)S(1)}, bf16[256,2048]{1,0:T(8,128)(2,1)S(1)}, u32[]{:S(2)}, u32[]{:S(2)}) collective-permute-start(bf16[256,2048]{1,0:T(8,128)(2,1)S(1)} %convolution_convert_fusion), channel_id=1, source_target_pairs={{0,1},{1,0},{2,3},{3,2},{4,5},{5,4},{6,7},{7,6},{8,9},{9,8},{10,11... | collective-permute-start | bytes 3145736 | tf_op jit(solution)/shard_map/ppermute | solution.py:27
  325.0 19.7 %collective-permute-start.21 = (bf16[256,1024]{1,0:T(8,128)(2,1)S(1)}, bf16[256,1024]{1,0:T(8,128)(2,1)}, u32[]{:S(2)}, u32[]{:S(2)}) collective-permute-start(bf16[256,1024]{1,0:T(8,128)(2,1)S(1)} %fusion.36), channel_id=1, source_target_pairs={{2,0},{4,2},{6,4},{8,6},{10,8},{12,10},{14,12},{16,14},{18,16},{20... | collective-permute-start | bytes 1572872 | tf_op jit(solution)/shard_map/ppermute | solution.py:22
  332.2 22.6 %collective-permute-start.19 = (bf16[256,1024]{1,0:T(8,128)(2,1)S(1)}, bf16[256,1024]{1,0:T(8,128)(2,1)S(1)}, u32[]{:S(2)}, u32[]{:S(2)}) collective-permute-start(bf16[256,1024]{1,0:T(8,128)(2,1)S(1)} %collective-permute-done.18), channel_id=1, source_target_pairs={{0,1},{1,0},{2,3},{3,2},{4,5},{5,4},{6,7},{7,6},{8,9},{9,8},{10,11... | collective-permute-start | bytes 1572872 | tf_op jit(solution)/shard_map/ppermute | solution.py:27
  344.8 20.4 %collective-permute-start.24 = (bf16[256,1024]{1,0:T(8,128)(2,1)}, bf16[256,1024]{1,0:T(8,128)(2,1)}, u32[]{:S(2)}, u32[]{:S(2)}) collective-permute-start(bf16[256,1024]{1,0:T(8,128)(2,1)} %fusion.38), channel_id=1, source_target_pairs={{2,0},{4,2},{6,4},{8,6},{10,8},{12,10},{14,12},{16,14},{18,16},{20... | collective-permute-start | bytes 1572872 | tf_op jit(solution)/shard_map/ppermute | solution.py:22
  349.6 22.0 %collective-permute-start.22 = (bf16[256,1024]{1,0:T(8,128)(2,1)}, bf16[256,1024]{1,0:T(8,128)(2,1)}, u32[]{:S(2)}, u32[]{:S(2)}) collective-permute-start(bf16[256,1024]{1,0:T(8,128)(2,1)} %collective-permute-done.21), channel_id=1, source_target_pairs={{0,1},{1,0},{2,3},{3,2},{4,5},{5,4},{6,7},{7,6},{8,9},{9,8},{10,11... | collective-permute-start | bytes 1572872 | tf_op jit(solution)/shard_map/ppermute | solution.py:27
  357.1 20.3 %collective-permute-start.26 = (bf16[256,1024]{1,0:T(8,128)(2,1)}, bf16[256,1024]{1,0:T(8,128)(2,1)}, u32[]{:S(2)}, u32[]{:S(2)}) collective-permute-start(bf16[256,1024]{1,0:T(8,128)(2,1)} %collective-permute-done.25), channel_id=1, source_target_pairs={{0,1},{1,0},{2,3},{3,2},{4,5},{5,4},{6,7},{7,6},{8,9},{9,8},{10,11... | collective-permute-start | bytes 1572872 | tf_op jit(solution)/shard_map/ppermute | solution.py:27
  371.5 15.4 %collective-permute-start.23 = (bf16[256,1024]{1,0:T(8,128)(2,1)S(1)}, bf16[256,1024]{1,0:T(8,128)(2,1)S(1)}, u32[]{:S(2)}, u32[]{:S(2)}) collective-permute-start(bf16[256,1024]{1,0:T(8,128)(2,1)S(1)} %convolution_convert_fusion.2), channel_id=1, source_target_pairs={{0,1},{1,0},{2,3},{3,2},{4,5},{5,4},{6,7},{7,6},{8,9},{9,8},{10,11... | collective-permute-start | bytes 1572872 | tf_op jit(solution)/shard_map/ppermute | solution.py:27
  404.1 14.7 %collective-permute-start.29 = (bf16[256,1024]{1,0:T(8,128)(2,1)S(1)}, bf16[256,1024]{1,0:T(8,128)(2,1)S(1)}, u32[]{:S(2)}, u32[]{:S(2)}) collective-permute-start(bf16[256,1024]{1,0:T(8,128)(2,1)S(1)} %convolution_convert_fusion.1), channel_id=1, source_target_pairs={{0,1},{1,0},{2,3},{3,2},{4,5},{5,4},{6,7},{7,6},{8,9},{9,8},{10,11... | collective-permute-start | bytes 1572872 | tf_op jit(solution)/shard_map/ppermute | solution.py:27
  (70 other events, 1309.3 us)

commit v3 on v2

--- a/solution.py
+++ b/solution.py
@@ -446,7 +446,7 @@
     entry_squares = sum_small(square_sum(entry)[None, :])
     entry_inverse = settled(lax.rsqrt(entry_squares / full_width + epsilon))
     pair = jnp.concatenate([first_saved, scaled(entry, first_gain_cols)], axis=0)
-    sent = other_products(pair, first_got, [entry_inverse])
+    sent = other_products(pair, first_got)
     mine = dot(fenced(pair, sent), first_up_own)
     got = collect(sent)
     pooled = fenced(pooled, sent)
@@ -514,7 +514,7 @@
     activated_late = fenced(entry_activated, late)
     if early < final:
         gots.append(first_out(early, final, activated_late))
-    ahead = [given, act_grad, *right, *(gots[-1] if early < final else ())]
+    ahead = [given, act_grad, *right]
     left = exchange_cols(returned[-1], ahead)[1:]
     pre_grad, along = gated(stored_mine, stored_got, inverse_rows[2:], act_grad, left, right)
     last_blocks, last_along = exchange_grad(pre_grad, along)

time: 425 us -> 425 us (level)
  no operation moved by 1% of the time
where the time goes in v3:
time: 425 us; the launch traced here: 420 us
  waiting for transfers between devices  259 us (61%)
  matrix products  51.2 us (12%)
  starting transfers between devices  47 us (11%)
  local copies, waits for them, and re-layouts  24.5 us (6%)
  other arithmetic  24.4 us (6%)
  Pallas kernels  11 us (3%)
    ppermute x28, waiting for transfers between devices, rotated(): lax.ppermute(value, 'tensor', [(i, (i + steps) % count) for i in range(co...  228 us
    ppermute x28, starting transfers between devices, rotated(): lax.ppermute(value, 'tensor', [(i, (i + steps) % count) for i in range(co...  32.6 us
    ppermute x5, waiting for transfers between devices, shifted(): lax.ppermute(value, axis, [(source, source + steps) for source in range(i...  31.4 us
    dot_general x21, matrix products, dot_t(): lax.dot_general(left, right, (((1,), (1,)), ((), ())), preferred_element_...  27.5 us
    dot_general x22, matrix products, dot(): return jnp.dot(left, right, preferred_element_type=f32)  23.7 us
    unnamed x120, local copies, waits for them, and re-layouts  22.5 us
    ppermute x5, starting transfers between devices, shifted(): lax.ppermute(value, axis, [(source, source + steps) for source in range(i...  14.4 us
  transfers between devices with their start and end apart: 33, of which 21 were waited for; matrix products, arithmetic and copies ran while one was open for 18% of the time, Pallas kernels for 2%

profile of v3, /device:TPU:16, one launch (start us, length us, event | category | flops | bytes accessed | tf_op | source)
XLA Modules:
  0.0 420.2 jit_solution(11243946095990695276)
XLA Ops:
  11.4 5.0 %fusion.8 = (f32[256]{0:T(256)S(1)}, bf16[1,256,4096]{2,1,0:T(8,128)(2,1)}, f32[256]{0:T(256)S(1)}, bf16[256,4096]{1,0:T(8,128)(2,1)S(1)}) fusion(bf16[1,256,4096]{2,1,0:T(8,128)(2,1)} %param.17, bf16[1,256,4096]{2,1,0:T(8,128)(2,1)} %param.18, pred[]{:T(512)S(6)} %eq.21, f32[4096]{0:T(1024)S(1)} %bitcast.129), kind=kLoop, calls=%fused_computation.25 | loop fusion | flops 9436672 | bytes 8407041 | tf_op jit(solution)/shard_map/reduce_sum | solution.py:296
  30.5 4.1 copy-done.8
  38.3 11.3 %collective-permute-done.1 = bf16[256,4096]{1,0:T(8,128)(2,1)} collective-permute-done((bf16[256,4096]{1,0:T(8,128)(2,1)}, bf16[256,4096]{1,0:T(8,128)(2,1)}, u32[]{:S(2)}, u32[]{:S(2)}) %collective-permute-start.1) | collective-permute-done | bytes 2097184 | tf_op jit(solution)/shard_map/ppermute | solution.py:27
  52.9 41.6 %collective-permute-done = bf16[2048,512]{1,0:T(8,128)(2,1)} collective-permute-done((bf16[2048,512]{1,0:T(8,128)(2,1)}, bf16[2048,512]{1,0:T(8,128)(2,1)}, u32[]{:S(2)}, u32[]{:S(2)}) %collective-permute-start) | collective-permute-done | bytes 2097184 | tf_op jit(solution)/shard_map/ppermute | solution.py:27
  101.3 38.0 %collective-permute-done.2 = bf16[2048,512]{1,0:T(8,128)(2,1)S(1)} collective-permute-done((bf16[2048,512]{1,0:T(8,128)(2,1)S(1)}, bf16[2048,512]{1,0:T(8,128)(2,1)S(1)}, u32[]{:S(2)}, u32[]{:S(2)}) %collective-permute-start.2) | collective-permute-done | bytes 2097184 | tf_op jit(solution)/shard_map/ppermute | solution.py:27
  148.6 13.2 %collective-permute-done.7 = bf16[1024,512]{1,0:T(8,128)(2,1)S(1)} collective-permute-done((bf16[1024,512]{1,0:T(8,128)(2,1)S(1)}, bf16[1024,512]{1,0:T(8,128)(2,1)S(1)}, u32[]{:S(2)}, u32[]{:S(2)}) %collective-permute-start.7) | collective-permute-done | bytes 1048608 | tf_op jit(solution)/shard_map/ppermute | solution.py:27
  163.3 3.8 pad_maximum_fusion.1
  172.1 19.3 %collective-permute-done.8 = bf16[1024,512]{1,0:T(8,128)(2,1)S(1)} collective-permute-done((bf16[1024,512]{1,0:T(8,128)(2,1)S(1)}, bf16[1024,512]{1,0:T(8,128)(2,1)S(1)}, u32[]{:S(2)}, u32[]{:S(2)}) %collective-permute-start.8) | collective-permute-done | bytes 1048608 | tf_op jit(solution)/shard_map/ppermute | solution.py:27
  194.7 8.0 %collective-permute-done.6 = bf16[256,1024]{1,0:T(8,128)(2,1)S(1)} collective-permute-done((bf16[256,1024]{1,0:T(8,128)(2,1)S(1)}, bf16[256,1024]{1,0:T(8,128)(2,1)S(1)}, u32[]{:S(2)}, u32[]{:S(2)}) %collective-permute-start.6) | collective-permute-done | bytes 524320 | tf_op jit(solution)/shard_map/ppermute | solution.py:27
  204.1 9.7 %collective-permute-done.9 = bf16[256,1024]{1,0:T(8,128)(2,1)S(1)} collective-permute-done((bf16[256,1024]{1,0:T(8,128)(2,1)S(1)}, bf16[256,1024]{1,0:T(8,128)(2,1)S(1)}, u32[]{:S(2)}, u32[]{:S(2)}) %collective-permute-start.9) | collective-permute-done | bytes 524320 | tf_op jit(solution)/shard_map/ppermute | solution.py:27
  215.4 9.7 %collective-permute-done.10 = bf16[256,1024]{1,0:T(8,128)(2,1)S(1)} collective-permute-done((bf16[256,1024]{1,0:T(8,128)(2,1)S(1)}, bf16[256,1024]{1,0:T(8,128)(2,1)S(1)}, u32[]{:S(2)}, u32[]{:S(2)}) %collective-permute-start.10) | collective-permute-done | bytes 524320 | tf_op jit(solution)/shard_map/ppermute | solution.py:27
  225.1 10.1 %collective-permute-done.11 = bf16[256,1024]{1,0:T(8,128)(2,1)S(1)} collective-permute-done((bf16[256,1024]{1,0:T(8,128)(2,1)S(1)}, bf16[256,1024]{1,0:T(8,128)(2,1)S(1)}, u32[]{:S(2)}, u32[]{:S(2)}) %collective-permute-start.11) | collective-permute-done | bytes 524320 | tf_op jit(solution)/shard_map/ppermute | solution.py:27
  241.8 23.7 %collective-permute-done.12 = bf16[256,4096]{1,0:T(8,128)(2,1)} collective-permute-done((bf16[256,4096]{1,0:T(8,128)(2,1)}, bf16[256,4096]{1,0:T(8,128)(2,1)}, u32[]{:S(2)}, u32[]{:S(2)}) %collective-permute-start.12) | collective-permute-done | bytes 2097184 | tf_op jit(solution)/shard_map/ppermute | solution.py:22
  272.3 21.2 %collective-permute-done.13 = bf16[2048,512]{1,0:T(8,128)(2,1)S(1)} collective-permute-done((bf16[2048,512]{1,0:T(8,128)(2,1)}, bf16[2048,512]{1,0:T(8,128)(2,1)S(1)}, u32[]{:S(2)}, u32[]{:S(2)}) %collective-permute-start.13) | collective-permute-done | bytes 2097184 | tf_op jit(solution)/shard_map/ppermute | solution.py:27
  301.8 7.4 %collective-permute-done.14.refs_0_ = bf16[512,512]{1,0:T(8,128)(2,1)S(1)} collective-permute-done((bf16[512,512]{1,0:T(8,128)(2,1)S(1)}, bf16[512,512]{1,0:T(8,128)(2,1)S(1)}, u32[]{:S(2)}, u32[]{:S(2)}) %collective-permute-start.14) | collective-permute-done | bytes 524320 | tf_op jit(solution)/shard_map/ppermute | solution.py:27
  314.5 6.4 %collective-permute-done.16 = bf16[256,512]{1,0:T(8,128)(2,1)S(1)} collective-permute-done((bf16[256,512]{1,0:T(8,128)(2,1)S(1)}, bf16[256,512]{1,0:T(8,128)(2,1)S(1)}, u32[]{:S(2)}, u32[]{:S(2)}) %collective-permute-start.16) | collective-permute-done | bytes 262176 | tf_op jit(solution)/shard_map/ppermute | solution.py:27
  334.1 7.7 %collective-permute-done.25 = bf16[256,1024]{1,0:T(8,128)(2,1)} collective-permute-done((bf16[256,1024]{1,0:T(8,128)(2,1)S(1)}, bf16[256,1024]{1,0:T(8,128)(2,1)}, u32[]{:S(2)}, u32[]{:S(2)}) %collective-permute-start.25) | collective-permute-done | bytes 524320 | tf_op jit(solution)/shard_map/ppermute | solution.py:22
  344.6 4.8 %collective-permute-start.24 = (bf16[256,1024]{1,0:T(8,128)(2,1)}, bf16[256,1024]{1,0:T(8,128)(2,1)}, u32[]{:S(2)}, u32[]{:S(2)}) collective-permute-start(bf16[256,1024]{1,0:T(8,128)(2,1)} %fusion.38), channel_id=1, source_target_pairs={{2,0},{4,2},{6,4},{8,6},{10,8},{12,10},{14,12},{16,14},{18,16},{20... | collective-permute-start | bytes 1572872 | tf_op jit(solution)/shard_map/ppermute | solution.py:22
  351.0 3.9 collective-permute-done.27.refs_1_
  360.3 3.7 fusion.86
  382.3 6.3 %collective-permute-done.23 = bf16[256,1024]{1,0:T(8,128)(2,1)S(1)} collective-permute-done((bf16[256,1024]{1,0:T(8,128)(2,1)S(1)}, bf16[256,1024]{1,0:T(8,128)(2,1)S(1)}, u32[]{:S(2)}, u32[]{:S(2)}) %collective-permute-start.23) | collective-permute-done | bytes 524320 | tf_op jit(solution)/shard_map/ppermute | solution.py:27
  389.3 8.9 %collective-permute-done.28.refs_1_ = bf16[256,1024]{1,0:T(8,128)(2,1)S(1)} collective-permute-done((bf16[256,1024]{1,0:T(8,128)(2,1)}, bf16[256,1024]{1,0:T(8,128)(2,1)S(1)}, u32[]{:S(2)}, u32[]{:S(2)}) %collective-permute-start.28) | collective-permute-done | bytes 524320 | tf_op jit(solution)/shard_map/ppermute | solution.py:27
  403.4 5.8 %collective-permute-done.31 = bf16[256,512]{1,0:T(8,128)(2,1)S(1)} collective-permute-done((bf16[256,512]{1,0:T(8,128)(2,1)S(1)}, bf16[256,512]{1,0:T(8,128)(2,1)S(1)}, u32[]{:S(2)}, u32[]{:S(2)}) %collective-permute-start.31) | collective-permute-done | bytes 262176 | tf_op jit(solution)/shard_map/ppermute | solution.py:27
  413.6 4.5 %collective-permute-done.29 = bf16[256,1024]{1,0:T(8,128)(2,1)S(1)} collective-permute-done((bf16[256,1024]{1,0:T(8,128)(2,1)S(1)}, bf16[256,1024]{1,0:T(8,128)(2,1)S(1)}, u32[]{:S(2)}, u32[]{:S(2)}) %collective-permute-start.29) | collective-permute-done | bytes 524320 | tf_op jit(solution)/shard_map/ppermute | solution.py:27
  (244 shorter events, 139.3 us)
Async XLA Ops:
  0.6 48.9 %collective-permute-start.1 = (bf16[256,4096]{1,0:T(8,128)(2,1)}, bf16[256,4096]{1,0:T(8,128)(2,1)}, u32[]{:S(2)}, u32[]{:S(2)}) collective-permute-start(bf16[256,4096]{1,0:T(8,128)(2,1)} %bitcast.156), channel_id=1, source_target_pairs={{0,1},{1,0},{2,3},{3,2},{4,5},{5,4},{6,7},{7,6},{8,9},{9,8},{10,11... | collective-permute-start | bytes 6291464 | tf_op jit(solution)/shard_map/ppermute | solution.py:27
  10.9 83.6 %collective-permute-start = (bf16[2048,512]{1,0:T(8,128)(2,1)}, bf16[2048,512]{1,0:T(8,128)(2,1)}, u32[]{:S(2)}, u32[]{:S(2)}) collective-permute-start(bf16[2048,512]{1,0:T(8,128)(2,1)} %get-tuple-element.63), channel_id=1, source_target_pairs={{0,1},{1,0},{2,3},{3,2},{4,5},{5,4},{6,7},{7,6},{8,9},{9,8},{10,11... | collective-permute-start | bytes 6291464 | tf_op jit(solution)/shard_map/ppermute | solution.py:27
  49.5 89.8 %collective-permute-start.2 = (bf16[2048,512]{1,0:T(8,128)(2,1)S(1)}, bf16[2048,512]{1,0:T(8,128)(2,1)S(1)}, u32[]{:S(2)}, u32[]{:S(2)}) collective-permute-start(bf16[2048,512]{1,0:T(8,128)(2,1)S(1)} %copy-done.26), channel_id=1, source_target_pairs={{0,1},{1,0},{2,3},{3,2},{4,5},{5,4},{6,7},{7,6},{8,9},{9,8},{10,11... | collective-permute-start | bytes 6291464 | tf_op jit(solution)/shard_map/ppermute | solution.py:27
  96.8 65.0 %collective-permute-start.7 = (bf16[1024,512]{1,0:T(8,128)(2,1)S(1)}, bf16[1024,512]{1,0:T(8,128)(2,1)S(1)}, u32[]{:S(2)}, u32[]{:S(2)}) collective-permute-start(bf16[1024,512]{1,0:T(8,128)(2,1)S(1)} %get-tuple-element.83), channel_id=1, source_target_pairs={{0,1},{1,0},{2,3},{3,2},{4,5},{5,4},{6,7},{7,6},{8,9},{9,8},{10,11... | collective-permute-start | bytes 3145736 | tf_op jit(solution)/shard_map/ppermute | solution.py:27
  142.4 26.2 %collective-permute-start.4 = (f32[3,256]{1,0:T(4,128)S(1)}, f32[3,256]{1,0:T(4,128)S(1)}, u32[]{:S(2)}, u32[]{:S(2)}) collective-permute-start(f32[3,256]{1,0:T(4,128)S(1)} %pad_maximum_fusion.3), channel_id=1, source_target_pairs={{0,1},{1,0},{2,3},{3,2},{4,5},{5,4},{6,7},{7,6},{8,9},{9,8},{10,11... | collective-permute-start | bytes 9224 | tf_op jit(solution)/shard_map/ppermute | solution.py:27
  143.9 25.0 %collective-permute-start.3 = (bf16[256,512]{1,0:T(8,128)(2,1)S(1)}, bf16[256,512]{1,0:T(8,128)(2,1)S(1)}, u32[]{:S(2)}, u32[]{:S(2)}) collective-permute-start(bf16[256,512]{1,0:T(8,128)(2,1)S(1)} %fusion.44), channel_id=1, source_target_pairs={{0,1},{1,0},{2,3},{3,2},{4,5},{5,4},{6,7},{7,6},{8,9},{9,8},{10,11... | collective-permute-start | bytes 786440 | tf_op jit(solution)/shard_map/ppermute | solution.py:27
  144.5 24.5 %collective-permute-start.5 = (f32[4,4096]{1,0:T(4,128)S(1)}, f32[4,4096]{1,0:T(4,128)S(1)}, u32[]{:S(2)}, u32[]{:S(2)}) collective-permute-start(f32[4,4096]{1,0:T(4,128)S(1)} %bitcast.135), channel_id=1, source_target_pairs={{0,1},{1,0},{2,3},{3,2},{4,5},{5,4},{6,7},{7,6},{8,9},{9,8},{10,11... | collective-permute-start | bytes 196616 | tf_op jit(solution)/shard_map/ppermute | solution.py:27
  161.8 29.6 %collective-permute-start.8 = (bf16[1024,512]{1,0:T(8,128)(2,1)S(1)}, bf16[1024,512]{1,0:T(8,128)(2,1)S(1)}, u32[]{:S(2)}, u32[]{:S(2)}) collective-permute-start(bf16[1024,512]{1,0:T(8,128)(2,1)S(1)} %get-tuple-element.84), channel_id=1, source_target_pairs={{0,1},{1,0},{2,3},{3,2},{4,5},{5,4},{6,7},{7,6},{8,9},{9,8},{10,11... | collective-permute-start | bytes 3145736 | tf_op jit(solution)/shard_map/ppermute | solution.py:27
  169.9 32.7 %collective-permute-start.6 = (bf16[256,1024]{1,0:T(8,128)(2,1)S(1)}, bf16[256,1024]{1,0:T(8,128)(2,1)S(1)}, u32[]{:S(2)}, u32[]{:S(2)}) collective-permute-start(bf16[256,1024]{1,0:T(8,128)(2,1)S(1)} %convolution_convert_fusion.6), channel_id=1, source_target_pairs={{0,1},{1,0},{2,3},{3,2},{4,5},{5,4},{6,7},{7,6},{8,9},{9,8},{10,11... | collective-permute-start | bytes 1572872 | tf_op jit(solution)/shard_map/ppermute | solution.py:27
  191.4 22.5 %collective-permute-start.9 = (bf16[256,1024]{1,0:T(8,128)(2,1)S(1)}, bf16[256,1024]{1,0:T(8,128)(2,1)S(1)}, u32[]{:S(2)}, u32[]{:S(2)}) collective-permute-start(bf16[256,1024]{1,0:T(8,128)(2,1)S(1)} %convolution_convert_fusion.5), channel_id=1, source_target_pairs={{0,1},{1,0},{2,3},{3,2},{4,5},{5,4},{6,7},{7,6},{8,9},{9,8},{10,11... | collective-permute-start | bytes 1572872 | tf_op jit(solution)/shard_map/ppermute | solution.py:27
  202.6 22.5 %collective-permute-start.10 = (bf16[256,1024]{1,0:T(8,128)(2,1)S(1)}, bf16[256,1024]{1,0:T(8,128)(2,1)S(1)}, u32[]{:S(2)}, u32[]{:S(2)}) collective-permute-start(bf16[256,1024]{1,0:T(8,128)(2,1)S(1)} %convolution_convert_fusion.4), channel_id=1, source_target_pairs={{0,1},{1,0},{2,3},{3,2},{4,5},{5,4},{6,7},{7,6},{8,9},{9,8},{10,11... | collective-permute-start | bytes 1572872 | tf_op jit(solution)/shard_map/ppermute | solution.py:27
  213.8 21.3 %collective-permute-start.11 = (bf16[256,1024]{1,0:T(8,128)(2,1)S(1)}, bf16[256,1024]{1,0:T(8,128)(2,1)S(1)}, u32[]{:S(2)}, u32[]{:S(2)}) collective-permute-start(bf16[256,1024]{1,0:T(8,128)(2,1)S(1)} %convolution_convert_fusion.3), channel_id=1, source_target_pairs={{0,1},{1,0},{2,3},{3,2},{4,5},{5,4},{6,7},{7,6},{8,9},{9,8},{10,11... | collective-permute-start | bytes 1572872 | tf_op jit(solution)/shard_map/ppermute | solution.py:27
  236.9 28.6 %collective-permute-start.12 = (bf16[256,4096]{1,0:T(8,128)(2,1)}, bf16[256,4096]{1,0:T(8,128)(2,1)}, u32[]{:S(2)}, u32[]{:S(2)}) collective-permute-start(bf16[256,4096]{1,0:T(8,128)(2,1)} %fusion.6), channel_id=1, source_target_pairs={{0,2},{2,4},{4,6},{6,8},{8,10},{10,12},{12,14},{14,16},{16,18},{18... | collective-permute-start | bytes 6291464 | tf_op jit(solution)/shard_map/ppermute | solution.py:22
  239.8 149.5 %collective-permute-start.30 = (bf16[256,512]{1,0:T(8,128)(2,1)}, bf16[256,512]{1,0:T(8,128)(2,1)S(1)}, u32[]{:S(2)}, u32[]{:S(2)}) collective-permute-start(bf16[256,512]{1,0:T(8,128)(2,1)} %fusion.45), channel_id=1, source_target_pairs={{0,1},{1,0},{2,3},{3,2},{4,5},{5,4},{6,7},{7,6},{8,9},{9,8},{10,11... | collective-permute-start | bytes 786440 | tf_op jit(solution)/shard_map/ppermute | solution.py:27
  241.3 52.2 %collective-permute-start.13 = (bf16[2048,512]{1,0:T(8,128)(2,1)}, bf16[2048,512]{1,0:T(8,128)(2,1)S(1)}, u32[]{:S(2)}, u32[]{:S(2)}) collective-permute-start(bf16[2048,512]{1,0:T(8,128)(2,1)} %copy-done.24), channel_id=1, source_target_pairs={{0,1},{1,0},{2,3},{3,2},{4,5},{5,4},{6,7},{7,6},{8,9},{9,8},{10,11... | collective-permute-start | bytes 6291464 | tf_op jit(solution)/shard_map/ppermute | solution.py:27
  270.2 31.5 %collective-permute-start.15 = (f32[1,256]{1,0:T(1,128)S(1)}, f32[1,256]{1,0:T(1,128)S(1)}, u32[]{:S(2)}, u32[]{:S(2)}) collective-permute-start(f32[1,256]{1,0:T(1,128)S(1)} %bitcast.150), channel_id=1, source_target_pairs={{0,1},{1,0},{2,3},{3,2},{4,5},{5,4},{6,7},{7,6},{8,9},{9,8},{10,11... | collective-permute-start | bytes 3080 | tf_op jit(solution)/shard_map/ppermute | solution.py:27
  312.9 36.6 %collective-permute-start.20 = (bf16[256,2048]{1,0:T(8,128)(2,1)S(1)}, bf16[256,2048]{1,0:T(8,128)(2,1)S(1)}, u32[]{:S(2)}, u32[]{:S(2)}) collective-permute-start(bf16[256,2048]{1,0:T(8,128)(2,1)S(1)} %convolution_convert_fusion), channel_id=1, source_target_pairs={{0,1},{1,0},{2,3},{3,2},{4,5},{5,4},{6,7},{7,6},{8,9},{9,8},{10,11... | collective-permute-start | bytes 3145736 | tf_op jit(solution)/shard_map/ppermute | solution.py:27
  325.0 19.7 %collective-permute-start.21 = (bf16[256,1024]{1,0:T(8,128)(2,1)S(1)}, bf16[256,1024]{1,0:T(8,128)(2,1)}, u32[]{:S(2)}, u32[]{:S(2)}) collective-permute-start(bf16[256,1024]{1,0:T(8,128)(2,1)S(1)} %fusion.36), channel_id=1, source_target_pairs={{2,0},{4,2},{6,4},{8,6},{10,8},{12,10},{14,12},{16,14},{18,16},{20... | collective-permute-start | bytes 1572872 | tf_op jit(solution)/shard_map/ppermute | solution.py:22
  332.1 22.8 %collective-permute-start.19 = (bf16[256,1024]{1,0:T(8,128)(2,1)S(1)}, bf16[256,1024]{1,0:T(8,128)(2,1)S(1)}, u32[]{:S(2)}, u32[]{:S(2)}) collective-permute-start(bf16[256,1024]{1,0:T(8,128)(2,1)S(1)} %collective-permute-done.18), channel_id=1, source_target_pairs={{0,1},{1,0},{2,3},{3,2},{4,5},{5,4},{6,7},{7,6},{8,9},{9,8},{10,11... | collective-permute-start | bytes 1572872 | tf_op jit(solution)/shard_map/ppermute | solution.py:27
  344.6 20.6 %collective-permute-start.24 = (bf16[256,1024]{1,0:T(8,128)(2,1)}, bf16[256,1024]{1,0:T(8,128)(2,1)}, u32[]{:S(2)}, u32[]{:S(2)}) collective-permute-start(bf16[256,1024]{1,0:T(8,128)(2,1)} %fusion.38), channel_id=1, source_target_pairs={{2,0},{4,2},{6,4},{8,6},{10,8},{12,10},{14,12},{16,14},{18,16},{20... | collective-permute-start | bytes 1572872 | tf_op jit(solution)/shard_map/ppermute | solution.py:22
  349.4 22.2 %collective-permute-start.22 = (bf16[256,1024]{1,0:T(8,128)(2,1)}, bf16[256,1024]{1,0:T(8,128)(2,1)}, u32[]{:S(2)}, u32[]{:S(2)}) collective-permute-start(bf16[256,1024]{1,0:T(8,128)(2,1)} %collective-permute-done.21), channel_id=1, source_target_pairs={{0,1},{1,0},{2,3},{3,2},{4,5},{5,4},{6,7},{7,6},{8,9},{9,8},{10,11... | collective-permute-start | bytes 1572872 | tf_op jit(solution)/shard_map/ppermute | solution.py:27
  357.2 20.3 %collective-permute-start.26 = (bf16[256,1024]{1,0:T(8,128)(2,1)}, bf16[256,1024]{1,0:T(8,128)(2,1)}, u32[]{:S(2)}, u32[]{:S(2)}) collective-permute-start(bf16[256,1024]{1,0:T(8,128)(2,1)} %collective-permute-done.25), channel_id=1, source_target_pairs={{0,1},{1,0},{2,3},{3,2},{4,5},{5,4},{6,7},{7,6},{8,9},{9,8},{10,11... | collective-permute-start | bytes 1572872 | tf_op jit(solution)/shard_map/ppermute | solution.py:27
  371.6 17.0 %collective-permute-start.23 = (bf16[256,1024]{1,0:T(8,128)(2,1)S(1)}, bf16[256,1024]{1,0:T(8,128)(2,1)S(1)}, u32[]{:S(2)}, u32[]{:S(2)}) collective-permute-start(bf16[256,1024]{1,0:T(8,128)(2,1)S(1)} %convolution_convert_fusion.2), channel_id=1, source_target_pairs={{0,1},{1,0},{2,3},{3,2},{4,5},{5,4},{6,7},{7,6},{8,9},{9,8},{10,11... | collective-permute-start | bytes 1572872 | tf_op jit(solution)/shard_map/ppermute | solution.py:27
  382.2 16.0 %collective-permute-start.28 = (bf16[256,1024]{1,0:T(8,128)(2,1)}, bf16[256,1024]{1,0:T(8,128)(2,1)S(1)}, u32[]{:S(2)}, u32[]{:S(2)}) collective-permute-start(bf16[256,1024]{1,0:T(8,128)(2,1)} %collective-permute-done.24), channel_id=1, source_target_pairs={{0,1},{1,0},{2,3},{3,2},{4,5},{5,4},{6,7},{7,6},{8,9},{9,8},{10,11... | collective-permute-start | bytes 1572872 | tf_op jit(solution)/shard_map/ppermute | solution.py:27
  (70 other events, 1297.6 us)
